TPU v7x, 128 devices: a whole 4x4x4 slice. The times are simulated.
128 devices in a mesh: gx: 4 (over z_hi, core), gy: 32 (over z_lo, x, y).
Axes of the slice: x: 4, y: 4, z: 4 (z_hi: 2, z_lo: 2; z = z_hi * 2 + z_lo), core: 2. Of those that a mesh axis runs over, the one named last changes fastest.
Arguments:
- node_feats: bfloat16 [163840, 512], P(('gx', 'gy')), may hold values from -6 to 6
- edge_feats: bfloat16 [524288, 512], P(('gx', 'gy')), may hold values from -6 to 6
- senders: int32 [524288], P(('gx', 'gy')), may hold values from 0 to 1791
- receivers: int32 [524288], P(('gx', 'gy')), may hold values from 0 to 1279, as said below
- send_lists: int32 [16384], P(('gx', 'gy')), may hold values from 0 to 1279
- coarse_edges: bfloat16 [20480, 512], P(('gx', 'gy')), may hold values from -6 to 6
- coarse_senders: int32 [20480], P(('gx', 'gy')), may hold values from 0 to 2559
- coarse_receivers: int32 [20480], P(('gx', 'gy')), may hold values from 0 to 2559, as said below
- edge_w1: bfloat16 [1536, 512], replicated, may hold values from -0.15625 to 0.15625
- edge_b1: float32 [512], replicated, may hold values from -4 to 4
- edge_w2: bfloat16 [512, 512], replicated, may hold values from -0.25 to 0.25
- edge_b2: float32 [512], replicated, may hold values from -3 to 3
- edge_gain: float32 [512], replicated, may hold values from 0.5 to 1.5
- edge_shift: float32 [512], replicated, may hold values from -3 to 3
- node_w1: bfloat16 [1024, 512], replicated, may hold values from -0.1875 to 0.1875
- node_b1: float32 [512], replicated, may hold values from -4 to 4
- node_w2: bfloat16 [512, 512], replicated, may hold values from -0.25 to 0.25
- node_b2: float32 [512], replicated, may hold values from -3 to 3
- node_gain: float32 [512], replicated, may hold values from 0.5 to 1.5
- node_shift: float32 [512], replicated, may hold values from -3 to 3
Outputs:
- new_nodes: bfloat16 [163840, 512], P(('gx', 'gy'))
- new_edges: bfloat16 [524288, 512], P(('gx', 'gy'))
- new_coarse: bfloat16 [20480, 512], P(('gx', 'gy'))
Inputs may be any that keep to these rules, and one draw needn't show every extreme that they name: Within one device the receivers start at 0, never fall, and rise by at most one from an edge to the next; within each aligned block of 128 of its edges they span at most 128 nodes. `coarse_receivers`: of the 160 coarse edges of one device, at most 3 have receivers c with the same c // 20.
All inputs are finite; a program needn't handle non-finite values.
Results may differ from a plain program's by a relative error of at most 0.003.
The roundings to bfloat16 on the way count: a program that leaves them out, or rounds other values in their place, can miss the bound.
Values may be sent and summed in bfloat16 or wider, within the bound.
A program may use at most 128 MiB of HBM per device.

v0:
```python
import math

import jax
import jax.numpy as jnp
from jax import lax
from jax.sharding import Mesh
from jax.sharding import PartitionSpec as P

NCD = 20
GX_GY = ("gx_0", "gx_1", "gy_0", "gy_1", "gy_2")
GX = ("gx_0", "gx_1")
GY = ("gy_0", "gy_1", "gy_2")


def with_halo(array, sides, width):
    edges = {}
    for axis, dim in sides:
        size, length = (lax.axis_size(axis), array.shape[dim])
        up = [(i, (i + 1) % size) for i in range(size)]
        last = lax.slice_in_dim(array, length - width, length, axis=dim)
        first = lax.slice_in_dim(array, 0, width, axis=dim)
        edges[dim] = (
            lax.ppermute(last, axis, up),
            lax.ppermute(first, axis, [(b, a) for a, b in up]),
        )
    done = []
    for _, dim in sides:
        low, high = edges[dim]
        around = [(width, width) if d in done else (0, 0) for d in range(array.ndim)]
        array = jnp.concatenate([jnp.pad(low, around), array, jnp.pad(high, around)], axis=dim)
        done.append(dim)
    return array


def piece_ends(length, count):
    unit = 8 if length >= 8 * count else 1
    return [length // unit * k // count * unit for k in range(1, count)]


def gather_in_order(array, axes, order):
    pieces = array
    for k in order:
        pieces = lax.all_gather(pieces, axes[k])
    done = order[::-1]
    back = [done.index(k) for k in range(len(axes))]
    pieces = pieces.transpose(*back, *range(len(axes), pieces.ndim))
    return pieces.reshape(-1, *array.shape)


def joined_along(pieces, dim):
    pieces = jnp.moveaxis(pieces, 0, dim)
    lengths = pieces.shape
    return pieces.reshape(*lengths[:dim], lengths[dim] * lengths[dim + 1], *lengths[dim + 2 :])


def spread_gather(array, axes, dim):
    widest = max(range(max(1, array.ndim - 1)), key=lambda d: array.shape[d])
    count, done = (len(axes), [])
    for first, piece in enumerate(
        jnp.split(array, piece_ends(array.shape[widest], count), axis=widest)
    ):
        if piece.size:
            order = [(first - k) % count for k in range(count)]
            done.append(gather_in_order(piece, axes, order))
    return joined_along(jnp.concatenate(done, axis=widest + 1), dim)


def sent_together(arrays, axis, split_dim, concat_dim, along):
    widths = [math.prod(a.shape[along:]) for a in arrays]
    both = jnp.concatenate(
        [a.reshape(*a.shape[:along], w) for a, w in zip(arrays, widths)], axis=along
    )
    out = lax.all_to_all(both, axis, split_axis=split_dim, concat_axis=concat_dim, tiled=True)
    pieces = jnp.split(out, [sum(widths[:k]) for k in range(1, len(widths))], axis=along)
    return tuple((b.reshape(*out.shape[:along], *a.shape[along:]) for a, b in zip(arrays, pieces)))


def layer_norm(values, gain_vec, shift_vec):
    row_mean = jnp.mean(values, -1, keepdims=True)
    centred = values - row_mean
    variance = jnp.mean(centred * centred, -1, keepdims=True)
    return centred * lax.rsqrt(variance + 1e-05) * gain_vec + shift_vec


def finish_edge(pre_act, edge_rows, w_second, b_second, gain_vec, shift_vec):
    hidden = jax.nn.silu(pre_act).astype(jnp.bfloat16)
    output = jnp.dot(hidden, w_second, preferred_element_type=jnp.float32) + b_second
    message = layer_norm(output, gain_vec, shift_vec)
    return (
        (edge_rows.astype(jnp.float32) + message).astype(jnp.bfloat16),
        message.astype(jnp.bfloat16),
    )


def on_device(
    node_feats,
    edge_feats,
    senders,
    receivers,
    send_lists,
    coarse_edges,
    coarse_senders,
    coarse_receivers,
    edge_w1,
    edge_b1,
    edge_w2,
    edge_b2,
    edge_gain,
    edge_shift,
    node_w1,
    node_b1,
    node_w2,
    node_b2,
    node_gain,
    node_shift,
):
    node_count = node_feats.shape[0]
    feat_width = node_feats.shape[1]
    boundary = node_feats[send_lists]
    padded = with_halo(boundary[None, None], ((GX, 0), (GY, 1)), 1)
    node_table = jnp.concatenate(
        [node_feats, padded[0, 1], padded[2, 1], padded[1, 0], padded[1, 2]], 0
    )
    group_count = edge_feats.shape[0] // 512
    edge_groups = edge_feats.reshape(group_count, 512, feat_width)
    send_groups = senders.reshape(group_count, 512)
    recv_groups = receivers.reshape(group_count, 512)
    window_size = min(512, node_count)
    window_ids = jnp.arange(window_size, dtype=jnp.int32)

    def group_step(summed, packed):
        edge_rows, send_ids, recv_ids = packed
        row_start = jnp.minimum(recv_ids[0], node_count - window_size)
        onehot = ((recv_ids - row_start)[None, :] == window_ids[:, None]).astype(jnp.bfloat16)
        node_window = lax.dynamic_slice_in_dim(node_feats, row_start, window_size, 0)
        recv_rows = jnp.einsum(
            "we,wd->ed", onehot, node_window, preferred_element_type=jnp.float32
        ).astype(jnp.bfloat16)
        send_rows = node_table[send_ids]
        inputs = jnp.concatenate([edge_rows, send_rows, recv_rows], 1)
        pre_act = jnp.dot(inputs, edge_w1, preferred_element_type=jnp.float32) + edge_b1
        updated, message = finish_edge(pre_act, edge_rows, edge_w2, edge_b2, edge_gain, edge_shift)
        partial_sum = jnp.dot(onehot, message, preferred_element_type=jnp.float32)
        window = lax.dynamic_slice_in_dim(summed, row_start, window_size, 0)
        summed = lax.dynamic_update_slice_in_dim(summed, window + partial_sum, row_start, 0)
        return (summed, updated)

    fine_sum, new_edges = lax.scan(
        group_step,
        jnp.zeros((node_count, feat_width), jnp.float32),
        (edge_groups, send_groups, recv_groups),
    )
    coarse_nodes = spread_gather(node_feats[:NCD], GX_GY, 0)
    coarse_in = jnp.concatenate(
        [coarse_edges, coarse_nodes[coarse_senders], coarse_nodes[coarse_receivers]], 1
    )
    coarse_pre = jnp.dot(coarse_in, edge_w1, preferred_element_type=jnp.float32) + edge_b1
    new_coarse, coarse_msg = finish_edge(
        coarse_pre, coarse_edges, edge_w2, edge_b2, edge_gain, edge_shift
    )
    ce_count = coarse_edges.shape[0]
    devices = lax.axis_size(GX_GY)
    slot_cap = max(2, (2 * ce_count + devices - 1) // devices)
    owners = coarse_receivers // NCD
    edge_ids = jnp.arange(ce_count, dtype=jnp.int32)
    earlier = (owners[None, :] == owners[:, None]) & (edge_ids[None, :] < edge_ids[:, None])
    rank_in_owner = jnp.sum(earlier.astype(jnp.int32), axis=1)
    slot_index = owners * slot_cap + rank_in_owner
    slot_range = jnp.arange(devices * slot_cap, dtype=jnp.int32)
    placing = slot_index[None, :] == slot_range[:, None]
    outbound = jnp.dot(
        placing.astype(jnp.bfloat16), coarse_msg, preferred_element_type=jnp.float32
    ).astype(jnp.bfloat16)
    local_rows = jnp.sum(jnp.where(placing, (coarse_receivers % NCD + 1)[None, :], 0), axis=1) - 1
    inbound, inbound_rows = sent_together(
        (outbound, local_rows.astype(jnp.bfloat16)), GX_GY, 0, 0, 1
    )
    owned_hot = (
        inbound_rows.astype(jnp.int32)[None, :] == jnp.arange(NCD, dtype=jnp.int32)[:, None]
    ).astype(jnp.bfloat16)
    owned_sum = jnp.dot(owned_hot, inbound, preferred_element_type=jnp.float32)
    fine_sum = jnp.concatenate([fine_sum[:NCD] + owned_sum, fine_sum[NCD:]], 0)
    node_in = jnp.concatenate([node_feats, fine_sum.astype(jnp.bfloat16)], 1)
    node_pre = jnp.dot(node_in, node_w1, preferred_element_type=jnp.float32) + node_b1
    node_hidden = jax.nn.silu(node_pre).astype(jnp.bfloat16)
    node_out = jnp.dot(node_hidden, node_w2, preferred_element_type=jnp.float32) + node_b2
    new_nodes = (
        node_feats.astype(jnp.float32) + layer_norm(node_out, node_gain, node_shift)
    ).astype(jnp.bfloat16)
    return (new_nodes, new_edges.reshape(group_count * 512, feat_width), new_coarse)


def solution(mesh):
    torus = Mesh(mesh.devices.reshape(2, 2, 2, 4, 4), ("gx_0", "gx_1", "gy_0", "gy_1", "gy_2"))
    in_specs = (
        P(GX_GY, None),
        P(GX_GY, None),
        P(GX_GY),
        P(GX_GY),
        P(GX_GY),
        P(GX_GY, None),
        P(GX_GY),
        P(GX_GY),
        P(),
        P(),
        P(),
        P(),
        P(),
        P(),
        P(),
        P(),
        P(),
        P(),
        P(),
        P(),
    )
    out_specs = (P(GX_GY, None), P(GX_GY, None), P(GX_GY, None))
    return jax.shard_map(
        on_device, mesh=torus, in_specs=in_specs, out_specs=out_specs, check_vma=False
    )
```

profile of v0, /device:TPU:1, one launch (start us, length us, event | category | flops | bytes accessed | tf_op | source)
XLA Modules:
  0.0 500.1 jit_solution(9397671210853544876)
XLA Ops:
  3.8 5.1 %collective-permute-start = (bf16[1,1,128,512]{3,2,1,0:T(8,128)(2,1)S(1)}, bf16[1,1,128,512]{3,2,1,0:T(8,128)(2,1)}, u32[]{:S(2)}, u32[]{:S(2)}) collective-permute-start(bf16[1,1,128,512]{3,2,1,0:T(8,128)(2,1)S(1)} %bitcast.110), channel_id=1, source_target_pairs={{0,32},{32,64},{64,96},{96,0},{1,33},{33,65},{65,97},{97,1},{2,34}... | collective-permute-start | bytes 393224 | tf_op jit(solution)/shard_map/ppermute | solution.py:23
  15.3 5.1 %all-gather.25 = bf16[2,4,512]{2,1,0:T(4,128)(2,1)S(1)} all-gather(bf16[1,4,512]{2,1,0:T(4,128)(2,1)S(1)} %get-tuple-element.252), channel_id=2, replica_groups=mesh['gx_0'=2,'gx_1'=2,'gy_0'=2,'gy_1'=4,'gy_2'=4] {'gx_0'}, dimensions={0}, use_global_device_ids=true | all-gather | bytes 12288 | tf_op jit(solution)/shard_map/all_gather | solution.py:43
  20.4 9.0 %all-gather.1 = bf16[8,4,512]{2,1,0:T(4,128)(2,1)S(1)} all-gather(bf16[2,4,512]{2,1,0:T(4,128)(2,1)S(1)} %all-gather.25), channel_id=3, replica_groups=mesh['gx_0'=2,'gx_1'=2,'gy_0'=2,'gy_1'=4,'gy_2'=4] {'gy_2'}, dimensions={0}, use_global_device_ids=true | all-gather | bytes 40960 | tf_op jit(solution)/shard_map/all_gather | solution.py:43
  29.4 9.5 %all-gather.2 = bf16[16,2,4,512]{3,2,1,0:T(4,128)(2,1)S(1)} all-gather(bf16[4,2,4,512]{3,2,1,0:T(4,128)(2,1)S(1)} %bitcast.114), channel_id=4, replica_groups=mesh['gx_0'=2,'gx_1'=2,'gy_0'=2,'gy_1'=4,'gy_2'=4] {'gy_1'}, dimensions={0}, use_global_device_ids=true | all-gather | bytes 163840 | tf_op jit(solution)/shard_map/all_gather | solution.py:43
  43.3 9.8 %all-gather.4 = bf16[4,4,4,2,4,512]{5,4,3,2,1,0:T(4,128)(2,1)S(1)} all-gather(bf16[2,4,4,2,4,512]{5,4,3,2,1,0:T(4,128)(2,1)S(1)} %bitcast.98), channel_id=6, replica_groups=mesh['gx_0'=2,'gx_1'=2,'gy_0'=2,'gy_1'=4,'gy_2'=4] {'gx_1'}, dimensions={0}, use_global_device_ids=true | all-gather | bytes 786432 | tf_op jit(solution)/shard_map/all_gather | solution.py:43
  55.3 4.9 all-gather.6
  60.3 9.0 %all-gather.7 = bf16[8,2,4,512]{3,2,1,0:T(4,128)(2,1)S(1)} all-gather(bf16[2,2,4,512]{3,2,1,0:T(4,128)(2,1)S(1)} %bitcast.117), channel_id=9, replica_groups=mesh['gx_0'=2,'gx_1'=2,'gy_0'=2,'gy_1'=4,'gy_2'=4] {'gy_2'}, dimensions={0}, use_global_device_ids=true | all-gather | bytes 81920 | tf_op jit(solution)/shard_map/all_gather | solution.py:43
  69.2 9.7 %all-gather.8 = bf16[16,2,2,4,512]{4,3,2,1,0:T(4,128)(2,1)S(1)} all-gather(bf16[4,2,2,4,512]{4,3,2,1,0:T(4,128)(2,1)S(1)} %bitcast.104), channel_id=10, replica_groups=mesh['gx_0'=2,'gx_1'=2,'gy_0'=2,'gy_1'=4,'gy_2'=4] {'gy_1'}, dimensions={0}, use_global_device_ids=true | all-gather | bytes 327680 | tf_op jit(solution)/shard_map/all_gather | solution.py:43
  78.9 6.2 %all-gather.9 = bf16[8,4,2,2,4,512]{5,4,3,2,1,0:T(4,128)(2,1)S(1)} all-gather(bf16[4,4,2,2,4,512]{5,4,3,2,1,0:T(4,128)(2,1)S(1)} %bitcast.97), channel_id=11, replica_groups=mesh['gx_0'=2,'gx_1'=2,'gy_0'=2,'gy_1'=4,'gy_2'=4] {'gy_0'}, dimensions={0}, use_global_device_ids=true | all-gather | bytes 786432 | tf_op jit(solution)/shard_map/all_gather | solution.py:43
  85.4 9.0 %all-gather.28 = bf16[4,4,512]{2,1,0:T(4,128)(2,1)S(1)} all-gather(bf16[1,4,512]{2,1,0:T(4,128)(2,1)S(1)} %get-tuple-element.249), channel_id=17, replica_groups=mesh['gx_0'=2,'gx_1'=2,'gy_0'=2,'gy_1'=4,'gy_2'=4] {'gy_1'}, dimensions={0}, use_global_device_ids=true | all-gather | bytes 20480 | tf_op jit(solution)/shard_map/all_gather | solution.py:43
  98.0 13.0 %all-gather.17 = bf16[4,4,4,512]{3,2,1,0:T(4,128)(2,1)S(1)} all-gather(bf16[2,4,4,512]{3,2,1,0:T(4,128)(2,1)S(1)} %bitcast.115), channel_id=19, replica_groups=mesh['gx_0'=2,'gx_1'=2,'gy_0'=2,'gy_1'=4,'gy_2'=4] {'gx_1'}, dimensions={0}, use_global_device_ids=true | all-gather | bytes 98304 | tf_op jit(solution)/shard_map/all_gather | solution.py:43
  110.9 6.2 %all-gather.18 = bf16[4,2,4,4,512]{4,3,2,1,0:T(4,128)(2,1)S(1)} all-gather(bf16[2,2,4,4,512]{4,3,2,1,0:T(4,128)(2,1)S(1)} %bitcast.106), channel_id=20, replica_groups=mesh['gx_0'=2,'gx_1'=2,'gy_0'=2,'gy_1'=4,'gy_2'=4] {'gx_0'}, dimensions={0}, use_global_device_ids=true | all-gather | bytes 196608 | tf_op jit(solution)/shard_map/all_gather | solution.py:43
  117.1 9.9 %all-gather.19 = bf16[8,2,2,4,4,512]{5,4,3,2,1,0:T(4,128)(2,1)S(1)} all-gather(bf16[2,2,2,4,4,512]{5,4,3,2,1,0:T(4,128)(2,1)S(1)} %bitcast.102), channel_id=21, replica_groups=mesh['gx_0'=2,'gx_1'=2,'gy_0'=2,'gy_1'=4,'gy_2'=4] {'gy_2'}, dimensions={0}, use_global_device_ids=true | all-gather | bytes 655360 | tf_op jit(solution)/shard_map/all_gather | solution.py:43
  130.7 6.7 %all-gather.11 = bf16[4,4,512]{2,1,0:T(4,128)(2,1)S(1)} all-gather(bf16[2,4,512]{2,1,0:T(4,128)(2,1)S(1)} %all-gather.27), channel_id=13, replica_groups=mesh['gx_0'=2,'gx_1'=2,'gy_0'=2,'gy_1'=4,'gy_2'=4] {'gx_1'}, dimensions={0}, use_global_device_ids=true | all-gather | bytes 24576 | tf_op jit(solution)/shard_map/all_gather | solution.py:43
  137.4 4.8 all-gather.12
  142.1 9.1 %all-gather.13 = bf16[8,2,2,4,512]{4,3,2,1,0:T(4,128)(2,1)S(1)} all-gather(bf16[2,2,2,4,512]{4,3,2,1,0:T(4,128)(2,1)S(1)} %bitcast.116), channel_id=15, replica_groups=mesh['gx_0'=2,'gx_1'=2,'gy_0'=2,'gy_1'=4,'gy_2'=4] {'gy_2'}, dimensions={0}, use_global_device_ids=true | all-gather | bytes 163840 | tf_op jit(solution)/shard_map/all_gather | solution.py:43
  151.2 10.7 %all-gather.14 = bf16[16,2,2,2,4,512]{5,4,3,2,1,0:T(4,128)(2,1)S(1)} all-gather(bf16[4,2,2,2,4,512]{5,4,3,2,1,0:T(4,128)(2,1)S(1)} %bitcast.101), channel_id=16, replica_groups=mesh['gx_0'=2,'gx_1'=2,'gy_0'=2,'gy_1'=4,'gy_2'=4] {'gy_1'}, dimensions={0}, use_global_device_ids=true | all-gather | bytes 655360 | tf_op jit(solution)/shard_map/all_gather | solution.py:43
  162.2 9.0 %all-gather.29 = bf16[4,4,512]{2,1,0:T(4,128)(2,1)S(1)} all-gather(bf16[1,4,512]{2,1,0:T(4,128)(2,1)S(1)} %get-tuple-element.248), channel_id=22, replica_groups=mesh['gx_0'=2,'gx_1'=2,'gy_0'=2,'gy_1'=4,'gy_2'=4] {'gy_2'}, dimensions={0}, use_global_device_ids=true | all-gather | bytes 20480 | tf_op jit(solution)/shard_map/all_gather | solution.py:43
  171.2 9.5 %all-gather.21 = bf16[16,4,512]{2,1,0:T(4,128)(2,1)S(1)} all-gather(bf16[4,4,512]{2,1,0:T(4,128)(2,1)S(1)} %all-gather.29), channel_id=23, replica_groups=mesh['gx_0'=2,'gx_1'=2,'gy_0'=2,'gy_1'=4,'gy_2'=4] {'gy_1'}, dimensions={0}, use_global_device_ids=true | all-gather | bytes 81920 | tf_op jit(solution)/shard_map/all_gather | solution.py:43
  184.5 15.1 %all-gather.23 = bf16[4,4,4,4,512]{4,3,2,1,0:T(4,128)(2,1)S(1)} all-gather(bf16[2,4,4,4,512]{4,3,2,1,0:T(4,128)(2,1)S(1)} %bitcast.103), channel_id=25, replica_groups=mesh['gx_0'=2,'gx_1'=2,'gy_0'=2,'gy_1'=4,'gy_2'=4] {'gx_1'}, dimensions={0}, use_global_device_ids=true | all-gather | bytes 393216 | tf_op jit(solution)/shard_map/all_gather | solution.py:43
  199.6 9.8 %all-gather.24 = bf16[4,2,4,4,4,512]{5,4,3,2,1,0:T(4,128)(2,1)} all-gather(bf16[2,2,4,4,4,512]{5,4,3,2,1,0:T(4,128)(2,1)S(1)} %bitcast.99), channel_id=26, replica_groups=mesh['gx_0'=2,'gx_1'=2,'gy_0'=2,'gy_1'=4,'gy_2'=4] {'gx_0'}, dimensions={0}, use_global_device_ids=true | all-gather | bytes 786432 | tf_op jit(solution)/shard_map/all_gather | solution.py:43
  209.4 11.1 %concatenate.26 = bf16[128,20,512]{2,1,0:T(8,128)(2,1)} concatenate(bf16[128,4,512]{2,1,0:T(4,128)(2,1)S(1)} %bitcast.91, bf16[128,4,512]{2,1,0:T(4,128)(2,1)S(1)} %bitcast.92, bf16[128,4,512]{2,1,0:T(4,128)(2,1)S(1)} %bitcast.94, bf16[128,4,512]{2,1,0:T(4,128)(2,1)S(1)} %bitcast.93, bf16[128,4,512]{2,1,0:T(4,128)(2,1)} %bitcast.95), dimensions={1} | concatenate | bytes 5242880 | tf_op jit(solution)/shard_map/concatenate | solution.py:65
  220.5 5.2 %reshape.159 = bf16[2560,512]{1,0:T(8,128)(2,1)} reshape(bf16[128,20,512]{2,1,0:T(8,128)(2,1)} %concatenate.26) | data formatting | bytes 5242880 | tf_op jit(solution)/shard_map/reshape | solution.py:53
  236.9 7.2 %all-to-all-start = ((bf16[128,3,513]{2,1,0:T(4,128)(2,1)}), bf16[128,3,513]{2,1,0:T(4,128)(2,1)}, u32[]{:S(2)}, u32[]{:S(2)}) async-start(bf16[128,3,513]{2,1,0:T(4,128)(2,1)} %pad_maximum_fusion.1), calls=%async_computation | async-start | bytes 1310720 | tf_op jit(solution)/shard_map/all_to_all | solution.py:73
  255.1 227.8 %while.13 = (s32[]{:T(128)}, f32[1280,512]{1,0:T(8,128)}, bf16[8,512,512]{2,1,0:T(8,128)(2,1)}, s32[8,512]{1,0:T(8,128)S(1)}, bf16[8,512,512]{2,1,0:T(8,128)(2,1...) while((s32[]{:T(128)}, f32[1280,512]{1,0:T(8,128)}, ...), condition=%wide.region_3.4_spmd.clone, body=%wide.region_0.3_spmd.clone.sunk | while | flops 1622412800 | bytes 22879148 | solution.py:148
  265.8 4.6 fusion.100
  294.5 4.6 fusion.100
  351.7 4.6 fusion.100
  380.4 4.6 fusion.100
  409.0 4.6 fusion.100
  437.6 4.6 fusion.100
  488.9 5.3 %fusion.77 = (f32[1280]{0:T(1024)S(1)}, f32[1280,512]{0,1:T(8,128)}) fusion(f32[512]{0:T(512)S(1)} %copy-done.24, bf16[512,512]{1,0:T(8,128)(2,1)S(1)} %copy-done.19, bf16[1024,512]{1,0:T(8,128)(2,1)S(1)} %copy-done, bf16[1260,512]{1,0:T(8,128)(2,1)} %slice.33, bf16[20,512]{1,0:T(8,128)(2,1)S(1)} %fusion.41, bf16[1280,512]{1,0:T(8,128)(2,1)S(1)} %copy-done.3, ...), kind=kOutput, calls=%fused_computation.119 | convolution fusion | flops 2026371840 | bytes 6824960 | tf_op jit(solution)/shard_map/dot_general | solution.py:186
  (346 shorter events, 245.8 us)
Async XLA Ops:
  0.6 488.2 %copy-start = (bf16[1024,512]{1,0:T(8,128)(2,1)S(1)}, bf16[1024,512]{1,0:T(8,128)(2,1)}, u32[]{:S(2)}) copy-start(bf16[1024,512]{1,0:T(8,128)(2,1)} %param.36) | copy-start | bytes 3145732
  3.8 245.8 %collective-permute-start = (bf16[1,1,128,512]{3,2,1,0:T(8,128)(2,1)S(1)}, bf16[1,1,128,512]{3,2,1,0:T(8,128)(2,1)}, u32[]{:S(2)}, u32[]{:S(2)}) collective-permute-start(bf16[1,1,128,512]{3,2,1,0:T(8,128)(2,1)S(1)} %bitcast.110), channel_id=1, source_target_pairs={{0,32},{32,64},{64,96},{96,0},{1,33},{33,65},{65,97},{97,1},{2,34}... | collective-permute-start | bytes 393224 | tf_op jit(solution)/shard_map/ppermute | solution.py:23
  8.8 241.7 %collective-permute-start.1 = (bf16[1,1,128,512]{3,2,1,0:T(8,128)(2,1)S(1)}, bf16[1,1,128,512]{3,2,1,0:T(8,128)(2,1)}, u32[]{:S(2)}, u32[]{:S(2)}) collective-permute-start(bf16[1,1,128,512]{3,2,1,0:T(8,128)(2,1)S(1)} %bitcast.111), channel_id=1, source_target_pairs={{32,0},{64,32},{96,64},{0,96},{33,1},{65,33},{97,65},{1,97},{34,2}... | collective-permute-start | bytes 393224 | tf_op jit(solution)/shard_map/ppermute | solution.py:24
  8.8 242.6 %collective-permute-start.2 = (bf16[1,1,128,512]{3,2,1,0:T(8,128)(2,1)S(1)}, bf16[1,1,128,512]{3,2,1,0:T(8,128)(2,1)}, u32[]{:S(2)}, u32[]{:S(2)}) collective-permute-start(bf16[1,1,128,512]{3,2,1,0:T(8,128)(2,1)S(1)} %bitcast.112), channel_id=1, source_target_pairs={{0,1},{1,2},{2,3},{3,4},{4,5},{5,6},{6,7},{7,8},{8,9},{9,10},{10,1... | collective-permute-start | bytes 393224 | tf_op jit(solution)/shard_map/ppermute | solution.py:23
  10.1 242.2 %collective-permute-start.3 = (bf16[1,1,128,512]{3,2,1,0:T(8,128)(2,1)S(1)}, bf16[1,1,128,512]{3,2,1,0:T(8,128)(2,1)}, u32[]{:S(2)}, u32[]{:S(2)}) collective-permute-start(bf16[1,1,128,512]{3,2,1,0:T(8,128)(2,1)S(1)} %bitcast.113), channel_id=1, source_target_pairs={{1,0},{2,1},{3,2},{4,3},{5,4},{6,5},{7,6},{8,7},{9,8},{10,9},{11,1... | collective-permute-start | bytes 393224 | tf_op jit(solution)/shard_map/ppermute | solution.py:24
  225.7 6.3 %copy-start.6 = (bf16[160,512]{1,0:T(8,128)(2,1)S(1)}, bf16[160,512]{1,0:T(8,128)(2,1)}, u32[]{:S(2)}) copy-start(bf16[160,512]{1,0:T(8,128)(2,1)} %param.27) | copy-start | bytes 491524
  225.7 6.3 %copy-start.18 = (bf16[512,512]{1,0:T(8,128)(2,1)S(1)}, bf16[512,512]{1,0:T(8,128)(2,1)}, u32[]{:S(2)}) copy-start(bf16[512,512]{1,0:T(8,128)(2,1)} %param.32) | copy-start | bytes 1572868
  225.7 6.3 %copy-start.20 = (f32[512]{0:T(512)S(1)}, f32[512]{0:T(512)}, u32[]{:S(2)}) copy-start(f32[512]{0:T(512)} %param.31) | copy-start | bytes 6148
  225.7 6.3 %copy-start.22 = (f32[512]{0:T(512)S(1)}, f32[512]{0:T(512)}, u32[]{:S(2)}) copy-start(f32[512]{0:T(512)} %param.33) | copy-start | bytes 6148
  234.4 11.2 %copy-start.12 = (f32[160]{0:T(256)}, f32[160]{0:T(256)S(1)}, u32[]{:S(2)}) copy-start(f32[160]{0:T(256)S(1)} %add_rsqrt_fusion.2) | copy-start | bytes 1924
  236.9 249.3 %all-to-all-start = ((bf16[128,3,513]{2,1,0:T(4,128)(2,1)}), bf16[128,3,513]{2,1,0:T(4,128)(2,1)}, u32[]{:S(2)}, u32[]{:S(2)}) async-start(bf16[128,3,513]{2,1,0:T(4,128)(2,1)} %pad_maximum_fusion.1), calls=%async_computation | async-start | bytes 1310720 | tf_op jit(solution)/shard_map/all_to_all | solution.py:73
  276.2 7.5 %copy-start.8 = (s32[8,512]{1,0:T(8,128)S(1)}, s32[8,512]{1,0:T(8,128)}, u32[]{:S(2)}) copy-start(s32[8,512]{1,0:T(8,128)} %copy-done.7) | copy-start | bytes 49156 | tf_op jit(solution)/shard_map/while
  276.2 7.5 %copy-start.10 = (s32[8,512]{1,0:T(8,128)S(1)}, s32[8,512]{1,0:T(8,128)}, u32[]{:S(2)}) copy-start(s32[8,512]{1,0:T(8,128)} %copy-done.9) | copy-start | bytes 49156 | tf_op jit(solution)/shard_map/while
  294.5 6.0 %copy-start.1 = (bf16[1,512,512]{1,2,0:T(8,128)(2,1)S(1)}, bf16[1,512,512]{1,2,0:T(8,128)(2,1)}, u32[]{:S(2)}) copy-start(bf16[1,512,512]{1,2,0:T(8,128)(2,1)} %copy.95) | copy-start | bytes 1572868 | tf_op jit(solution)/shard_map/while
  304.9 7.5 %copy-start.8 = (s32[8,512]{1,0:T(8,128)S(1)}, s32[8,512]{1,0:T(8,128)}, u32[]{:S(2)}) copy-start(s32[8,512]{1,0:T(8,128)} %copy-done.7) | copy-start | bytes 49156 | tf_op jit(solution)/shard_map/while
  304.9 7.5 %copy-start.10 = (s32[8,512]{1,0:T(8,128)S(1)}, s32[8,512]{1,0:T(8,128)}, u32[]{:S(2)}) copy-start(s32[8,512]{1,0:T(8,128)} %copy-done.9) | copy-start | bytes 49156 | tf_op jit(solution)/shard_map/while
  333.5 7.5 %copy-start.8 = (s32[8,512]{1,0:T(8,128)S(1)}, s32[8,512]{1,0:T(8,128)}, u32[]{:S(2)}) copy-start(s32[8,512]{1,0:T(8,128)} %copy-done.7) | copy-start | bytes 49156 | tf_op jit(solution)/shard_map/while
  333.5 7.5 %copy-start.10 = (s32[8,512]{1,0:T(8,128)S(1)}, s32[8,512]{1,0:T(8,128)}, u32[]{:S(2)}) copy-start(s32[8,512]{1,0:T(8,128)} %copy-done.9) | copy-start | bytes 49156 | tf_op jit(solution)/shard_map/while
  351.7 6.0 %copy-start.1 = (bf16[1,512,512]{1,2,0:T(8,128)(2,1)S(1)}, bf16[1,512,512]{1,2,0:T(8,128)(2,1)}, u32[]{:S(2)}) copy-start(bf16[1,512,512]{1,2,0:T(8,128)(2,1)} %copy.95) | copy-start | bytes 1572868 | tf_op jit(solution)/shard_map/while
  362.1 7.6 %copy-start.8 = (s32[8,512]{1,0:T(8,128)S(1)}, s32[8,512]{1,0:T(8,128)}, u32[]{:S(2)}) copy-start(s32[8,512]{1,0:T(8,128)} %copy-done.7) | copy-start | bytes 49156 | tf_op jit(solution)/shard_map/while
  362.1 7.6 %copy-start.10 = (s32[8,512]{1,0:T(8,128)S(1)}, s32[8,512]{1,0:T(8,128)}, u32[]{:S(2)}) copy-start(s32[8,512]{1,0:T(8,128)} %copy-done.9) | copy-start | bytes 49156 | tf_op jit(solution)/shard_map/while
  380.4 6.0 %copy-start.1 = (bf16[1,512,512]{1,2,0:T(8,128)(2,1)S(1)}, bf16[1,512,512]{1,2,0:T(8,128)(2,1)}, u32[]{:S(2)}) copy-start(bf16[1,512,512]{1,2,0:T(8,128)(2,1)} %copy.95) | copy-start | bytes 1572868 | tf_op jit(solution)/shard_map/while
  390.8 7.5 %copy-start.8 = (s32[8,512]{1,0:T(8,128)S(1)}, s32[8,512]{1,0:T(8,128)}, u32[]{:S(2)}) copy-start(s32[8,512]{1,0:T(8,128)} %copy-done.7) | copy-start | bytes 49156 | tf_op jit(solution)/shard_map/while
  390.8 7.5 %copy-start.10 = (s32[8,512]{1,0:T(8,128)S(1)}, s32[8,512]{1,0:T(8,128)}, u32[]{:S(2)}) copy-start(s32[8,512]{1,0:T(8,128)} %copy-done.9) | copy-start | bytes 49156 | tf_op jit(solution)/shard_map/while
  409.0 6.0 %copy-start.1 = (bf16[1,512,512]{1,2,0:T(8,128)(2,1)S(1)}, bf16[1,512,512]{1,2,0:T(8,128)(2,1)}, u32[]{:S(2)}) copy-start(bf16[1,512,512]{1,2,0:T(8,128)(2,1)} %copy.95) | copy-start | bytes 1572868 | tf_op jit(solution)/shard_map/while
  419.4 7.5 %copy-start.8 = (s32[8,512]{1,0:T(8,128)S(1)}, s32[8,512]{1,0:T(8,128)}, u32[]{:S(2)}) copy-start(s32[8,512]{1,0:T(8,128)} %copy-done.7) | copy-start | bytes 49156 | tf_op jit(solution)/shard_map/while
  419.4 7.5 %copy-start.10 = (s32[8,512]{1,0:T(8,128)S(1)}, s32[8,512]{1,0:T(8,128)}, u32[]{:S(2)}) copy-start(s32[8,512]{1,0:T(8,128)} %copy-done.9) | copy-start | bytes 49156 | tf_op jit(solution)/shard_map/while
  437.6 6.0 %copy-start.1 = (bf16[1,512,512]{1,2,0:T(8,128)(2,1)S(1)}, bf16[1,512,512]{1,2,0:T(8,128)(2,1)}, u32[]{:S(2)}) copy-start(bf16[1,512,512]{1,2,0:T(8,128)(2,1)} %copy.95) | copy-start | bytes 1572868 | tf_op jit(solution)/shard_map/while
  448.0 6.9 %copy-start.8 = (s32[8,512]{1,0:T(8,128)S(1)}, s32[8,512]{1,0:T(8,128)}, u32[]{:S(2)}) copy-start(s32[8,512]{1,0:T(8,128)} %copy-done.7) | copy-start | bytes 49156 | tf_op jit(solution)/shard_map/while
  448.0 6.9 %copy-start.10 = (s32[8,512]{1,0:T(8,128)S(1)}, s32[8,512]{1,0:T(8,128)}, u32[]{:S(2)}) copy-start(s32[8,512]{1,0:T(8,128)} %copy-done.9) | copy-start | bytes 49156 | tf_op jit(solution)/shard_map/while
  476.0 6.9 %copy-start.8 = (s32[8,512]{1,0:T(8,128)S(1)}, s32[8,512]{1,0:T(8,128)}, u32[]{:S(2)}) copy-start(s32[8,512]{1,0:T(8,128)} %copy-done.7) | copy-start | bytes 49156 | tf_op jit(solution)/shard_map/while
  476.0 6.9 %copy-start.10 = (s32[8,512]{1,0:T(8,128)S(1)}, s32[8,512]{1,0:T(8,128)}, u32[]{:S(2)}) copy-start(s32[8,512]{1,0:T(8,128)} %copy-done.9) | copy-start | bytes 49156 | tf_op jit(solution)/shard_map/while
  (48 other events, 211.2 us)
where the time goes:
time: 504 us; the launch traced here: 500 us
  blocking collectives  193 us (38%)
  local copies, waits for them, and re-layouts  135 us (27%)
  matrix products  90.2 us (18%)
  other arithmetic  47.1 us (9%)
  starting transfers between devices  18 us (4%)
  loops' own time  15.9 us (3%)
    all_gather x25, blocking collectives, gather_in_order(): pieces = lax.all_gather(pieces, axes[k])  193 us
    dot_general x9, matrix products, finish_edge(): jnp.dot(hidden, w_second, preferred_element_type=jnp.float32) + b_second  39 us
    dynamic_update_slice x8, local copies, waits for them, and re-layouts, group_step(): lax.dynamic_update_slice_in_dim(summed, window + partial_sum, row_start, 0)  33.4 us
    dot_general x8, matrix products, group_step(): partial_sum = jnp.dot(onehot, message, preferred_element_type=jnp.float32)  25.5 us
    gather x16, local copies, waits for them, and re-layouts, group_step(): send_rows = node_table[send_ids]  23.8 us
    dot_general x8, matrix products, group_step(): jnp.einsum('we,wd->ed', onehot, node_window, preferred_element_type=jnp.f...  19.1 us
    broadcast_in_dim x9, other arithmetic, on_device(): lax.scan(group_step, jnp.zeros((node_count, feat_width), jnp.float32), (e...  18.5 us
    dynamic_slice x16, local copies, waits for them, and re-layouts, on_device(): lax.scan(group_step, jnp.zeros((node_count, feat_width), jnp.float32), (e...  16.8 us
  transfers between devices with their start and end apart: 5, of which 0 were waited for; matrix products, arithmetic and copies ran while one was open for 51% of the time, Pallas kernels for 0%

commit v1 on v0

v1 whole, which is shorter than its diff:
```python
import functools

import jax
import jax.numpy as jnp
from jax import lax
from jax.experimental import pallas as pl
from jax.experimental.pallas import tpu as pltpu
from jax.sharding import PartitionSpec as P

BF, F32 = jnp.bfloat16, jnp.float32
BLK = 256
WIN = 264


def norm_rows(x, gain, shift):
    mean = jnp.mean(x, -1, keepdims=True)
    c = x - mean
    var = jnp.mean(c * c, -1, keepdims=True)
    return c * lax.rsqrt(var + 1e-05) * gain + shift


def silu(x):
    t = 0.5 * x
    return t + t * jnp.tanh(t)


def fine_kernel(
    snd, rcv,
    edges, node_ref, halo_ref, rcol_a, w1, b1, w2, b2, gain, shift,
    nw1, nb1, nw2, nb2, ngain, nshift,
    new_edges, new_nodes, head,
    p_snd, p_rcv, g_a, g_b, fsum,
    *, esteps, nodes, do_gather=True, do_seg=True, do_mlp=True,
):
    i = pl.program_id(0)
    D = 512

    def gather(block, g):
        if not do_gather:
            return
        base = block * BLK
        for e in range(BLK):
            s = pl.multiple_of(snd[base + e] * 4, 4)
            r = pl.multiple_of(rcv[base + e] * 4, 4)
            g[pl.ds(4 * e, 4), :] = p_snd[pl.ds(s, 4), :] + p_rcv[pl.ds(r, 4), :]

    def project(rows, w_lo, w_hi, table, at, bias):
        n = rows.shape[0]
        for j in range(4):
            v = jnp.dot(rows, w1[w_lo:w_hi, 128 * j:128 * (j + 1)], preferred_element_type=F32)
            if bias is not None:
                v = v + bias[:, 128 * j:128 * (j + 1)]
            table[pl.ds(at * 4 + j, n, stride=4), :] = v

    @pl.when(i == 0)
    def _():
        fsum[...] = jnp.zeros_like(fsum)
        for c in range(nodes // 256):
            rows = node_ref[c * 256:(c + 1) * 256, :]
            project(rows, 512, 1024, p_snd, c * 256, None)
            project(rows, 1024, 1536, p_rcv, c * 256, b1[...])
        for c in range(2):
            project(halo_ref[c * 256:(c + 1) * 256, :], 512, 1024, p_snd, nodes + c * 256, None)
        gather(0, g_a)

    def compute(k, g, block):
        x = edges[pl.ds(k * BLK, BLK), :]
        acc = jnp.dot(x, w1[0:512, :], preferred_element_type=F32)
        pre = acc + jnp.concatenate([g[pl.ds(j, BLK, stride=4), :] for j in range(4)], 1)
        if do_mlp:
            h = silu(pre).astype(BF)
            y = jnp.dot(h, w2[...], preferred_element_type=F32) + b2[...]
            m = norm_rows(y, gain[...], shift[...])
        else:
            m = pre
        new_edges[pl.ds(k * BLK, BLK), :] = (x.astype(F32) + m).astype(BF)
        if do_seg:
            start = pl.multiple_of((rcv[block * BLK] // 8) * 8, 8)
            ids = rcol_a[0, k:k + 1, :]
            hot = (ids - start == lax.broadcasted_iota(jnp.int32, (WIN, BLK), 0)).astype(F32).astype(BF)
            part = jnp.dot(hot, m.astype(BF), preferred_element_type=F32)
            fsum[pl.ds(start, WIN), :] += part

    @pl.when(i < esteps)
    def _():
        gather(2 * i + 1, g_b)
        compute(0, g_a, 2 * i)
        gather(jnp.minimum(2 * i + 2, 2 * esteps - 1), g_a)
        compute(1, g_b, 2 * i + 1)

    @pl.when(i >= esteps)
    def _():
        c = i - esteps
        rows = node_ref[pl.ds(pl.multiple_of(c * 256, 256), 256), :]
        agg = fsum[pl.ds(pl.multiple_of(c * 256, 256), 256), :]
        pre = (
            jnp.dot(rows, nw1[0:512, :], preferred_element_type=F32)
            + jnp.dot(agg.astype(BF), nw1[512:1024, :], preferred_element_type=F32)
            + nb1[...]
        )
        y = jnp.dot(silu(pre).astype(BF), nw2[...], preferred_element_type=F32) + nb2[...]
        new_nodes[...] = (rows.astype(F32) + norm_rows(y, ngain[...], nshift[...])).astype(BF)

    @pl.when(i == esteps)
    def _():
        head[...] = fsum[0:32, :]


def fine_call(snd, rcv, edges, nodes_a, halo, w1, b1, w2, b2, gain, shift, nw1, nb1, nw2, nb2, ngain, nshift, **kw):
    E, D = edges.shape
    N = nodes_a.shape[0]
    esteps = E // (2 * BLK)
    nsteps = N // 256
    rc = rcv.reshape(esteps, 2, BLK)
    row = lambda v: v.reshape(1, D)
    full = lambda s: pl.BlockSpec(s, lambda i, *_: (0,) * len(s))
    return pl.pallas_call(
        functools.partial(fine_kernel, esteps=esteps, nodes=N, **kw),
        out_shape=(
            jax.ShapeDtypeStruct((E, D), BF),
            jax.ShapeDtypeStruct((N, D), BF),
            jax.ShapeDtypeStruct((32, D), F32),
        ),
        grid_spec=pltpu.PrefetchScalarGridSpec(
            num_scalar_prefetch=2,
            grid=(esteps + nsteps,),
            in_specs=[
                pl.BlockSpec((2 * BLK, D), lambda i, *_: (jnp.minimum(i, esteps - 1), 0)),
                full((N, D)), full(halo.shape),
                pl.BlockSpec((1, 2, BLK), lambda i, *_: (jnp.minimum(i, esteps - 1), 0, 0)),
                full((3 * D, D)), full((1, D)), full((D, D)), full((1, D)), full((1, D)), full((1, D)),
                full((2 * D, D)), full((1, D)), full((D, D)), full((1, D)), full((1, D)), full((1, D)),
            ],
            out_specs=(
                pl.BlockSpec((2 * BLK, D), lambda i, *_: (jnp.minimum(i, esteps - 1), 0)),
                pl.BlockSpec((256, D), lambda i, *_: (jnp.maximum(i - esteps, 0), 0)),
                full((32, D)),
            ),
            scratch_shapes=[
                pltpu.VMEM(((N + halo.shape[0]) * 4, 128), F32),
                pltpu.VMEM((N * 4, 128), F32),
                pltpu.VMEM((BLK * 4, 128), F32),
                pltpu.VMEM((BLK * 4, 128), F32),
                pltpu.VMEM((N + WIN, D), F32),
            ],
        ),
        compiler_params=pltpu.CompilerParams(vmem_limit_bytes=60 * 2**20, dimension_semantics=("arbitrary",)),
        cost_estimate=pl.CostEstimate(flops=10 * 10**9, bytes_accessed=14 * 10**6, transcendentals=3 * 10**6),
        name="fine",
    )(snd, rcv, edges, nodes_a, halo, rc, w1, row(b1), w2, row(b2), row(gain), row(shift),
      nw1, row(nb1), nw2, row(nb2), row(ngain), row(nshift))


MESH = pl.DeviceIdType.MESH
NCD = 20
PIECES = ((0, 32), (32, 32), (64, 16))


def coords(a, b):
    return lax.rem(a, 2), (a // 2) * 2 + b // 16, lax.rem(b // 4, 4), lax.rem(b, 4)


def device_at(core, z, x, y):
    return ((z // 2) * 2 + core, lax.rem(z, 2) * 16 + x * 4 + y)


ORDERS = ((3, 2, 1), (2, 1, 3), (1, 3, 2))


def comm_kernel(
    node_ref, lists,
    halo, buf0, buf1, buf2,
    bound, head32,
    send_sem, recv_sem, csend_sem, crecv_sem, hsend_sem, hrecv_sem,
):
    a, b = lax.axis_index("gx"), lax.axis_index("gy")
    me = coords(a, b)
    core = me[0]
    bufs = (buf0, buf1, buf2)

    def peer(axis, step):
        c = list(me)
        c[axis] = lax.rem(c[axis] + step, 4)
        return device_at(*c)

    sibling = (a + 1 - 2 * core, b)
    halo_to = (
        (lax.rem(a + 1, 4), b), (lax.rem(a + 3, 4), b),
        (a, lax.rem(b + 1, 32)), (a, lax.rem(b + 31, 32)),
    )
    partners = [peer(axis, s) for axis in (1, 2, 3) for s in (1, 2, 3)] + [sibling] + list(halo_to)
    barrier = pltpu.get_barrier_semaphore()
    for p in partners:
        pl.semaphore_signal(barrier, inc=1, device_id=p, device_id_type=MESH)

    own = node_ref[0:32, :].astype(F32)
    for j in range(4):
        head32[pl.ds(j, 32, stride=4), :] = own[:, 128 * j:128 * (j + 1)]

    def slot(p):
        o = ORDERS[p]
        return ((core * 4 + me[o[2]]) * 4 + me[o[1]]) * 4 + me[o[0]]

    for p, (r0, n) in enumerate(PIECES):
        bufs[p][slot(p)] = head32[r0:r0 + n, :].astype(BF)

    hot = (lax.broadcasted_iota(jnp.int32, (node_ref.shape[0], 128), 0) == lists[...]).astype(F32).astype(BF)
    bound[...] = lax.dot_general(
        hot, node_ref[...], (((0,), (0,)), ((), ())), preferred_element_type=F32).astype(BF)

    pl.semaphore_wait(barrier, len(partners))

    def hop(p, stage, step):
        o = ORDERS[p]
        size = 4 ** stage
        first = slot(p) // size * size
        part = bufs[p].at[pl.ds(first, size)]
        k = (p * 3 + stage) * 3 + step - 1
        return pltpu.make_async_remote_copy(
            src_ref=part, dst_ref=part, send_sem=send_sem.at[k], recv_sem=recv_sem.at[k],
            device_id=peer(o[stage], step), device_id_type=MESH)

    def across(p, step):
        o = ORDERS[p]
        first = (core * 4 + lax.rem(me[o[2]] + 4 - step, 4)) * 16
        part = bufs[p].at[pl.ds(first, 16)]
        k = p * 4 + step
        return pltpu.make_async_remote_copy(
            src_ref=part, dst_ref=part, send_sem=csend_sem.at[k], recv_sem=crecv_sem.at[k],
            device_id=sibling, device_id_type=MESH)

    started = []

    def go(copy):
        copy.start()
        started.append(copy)
        return copy

    stage = [[go(hop(p, 0, s)) for s in (2, 1, 3)] for p in range(3)]
    halos = []
    for k, to in enumerate(halo_to):
        halos.append(go(pltpu.make_async_remote_copy(
            src_ref=bound, dst_ref=halo.at[pl.ds(128 * k, 128)], send_sem=hsend_sem.at[k], recv_sem=hrecv_sem.at[k],
            device_id=to, device_id_type=MESH)))
    nxt = []
    for p in range(3):
        for c in stage[p]:
            c.wait_recv()
        nxt.append([go(hop(p, 1, s)) for s in (2, 1, 3)])
    stage, nxt, cross = nxt, [], []
    for p in range(3):
        for c in stage[p]:
            c.wait_recv()
        nxt.append([go(hop(p, 2, s)) for s in (2, 1, 3)])
        cross.append(go(across(p, 0)))
    for i, s in enumerate((2, 1, 3)):
        for p in range(3):
            nxt[p][i].wait_recv()
            cross.append(go(across(p, s)))
    for c in cross:
        c.wait_recv()

    for h in halos:
        h.wait_recv()
    for k in started:
        k.wait_send()


def coarse_kernel(
    csnd, crcv,
    buf0, buf1, buf2, cedges, crow, w1, b1, w2, b2, gain, shift,
    new_coarse, outbound,
    table, rows_s, rows_r, wide,
):
    bufs = (buf0, buf1, buf2)

    @pl.loop(0, 128)
    def _(q):
        c, u, v, w = q // 64, lax.rem(q // 16, 4), lax.rem(q // 4, 4), lax.rem(q, 4)
        for p, (r0, n) in enumerate(PIECES):
            pos = {ORDERS[p][2]: u, ORDERS[p][1]: v, ORDERS[p][0]: w}
            aa, bb = device_at(c, pos[1], pos[2], pos[3])
            at = pl.multiple_of((aa * 32 + bb) * 80 + r0, 8)
            table[pl.ds(at, n), :] = bufs[p][q].astype(F32)

    ce = cedges.shape[0]
    for e in range(ce):
        rows_s[pl.ds(4 * e, 4), :] = table[pl.ds(pl.multiple_of(csnd[e] * 4, 4), 4), :]
        rows_r[pl.ds(4 * e, 4), :] = table[pl.ds(pl.multiple_of(crcv[e] * 4, 4), 4), :]
    x = cedges[...]
    take = lambda ref: jnp.concatenate([ref[pl.ds(j, ce, stride=4), :] for j in range(4)], 1).astype(BF)
    pre = (
        jnp.dot(x, w1[0:512, :], preferred_element_type=F32)
        + jnp.dot(take(rows_s), w1[512:1024, :], preferred_element_type=F32)
        + jnp.dot(take(rows_r), w1[1024:1536, :], preferred_element_type=F32)
        + b1[...]
    )
    y = jnp.dot(silu(pre).astype(BF), w2[...], preferred_element_type=F32) + b2[...]
    m = norm_rows(y, gain[...], shift[...])
    new_coarse[...] = (x.astype(F32) + m).astype(BF)
    mb = m.astype(BF)

    c = crow[...]
    owner = lax.shift_right_logical(c * 52429, 20)
    local = c - owner * NCD
    iota = lambda shape, d: lax.broadcasted_iota(jnp.int32, shape, d)
    own_hot = (iota((128, ce), 0) == owner).astype(F32)
    before = (iota((ce, ce), 0) < iota((ce, ce), 1)).astype(F32).astype(BF)
    counts = jnp.dot(own_hot.astype(BF), before, preferred_element_type=F32)
    rank = jnp.sum(own_hot * counts, axis=0, keepdims=True)
    for s in range(3):
        placed = jnp.where(rank == s, own_hot, 0.0).astype(BF)
        got = jnp.dot(placed, mb, preferred_element_type=F32)
        for j in range(4):
            wide[pl.ds(4 * s + j, 128, stride=16), :] = got[:, 128 * j:128 * (j + 1)]
    tags = (iota((128, ce), 0).astype(F32) == rank * 32.0 + local.astype(F32)).astype(F32).astype(BF)
    wide[pl.ds(12, 128, stride=16), :] = lax.dot_general(
        own_hot.astype(BF), tags, (((1,), (1,)), ((), ())), preferred_element_type=F32)
    for j in range(1, 4):
        wide[pl.ds(12 + j, 128, stride=16), :] = jnp.zeros((128, 128), F32)
    outbound[...] = wide[...].astype(BF)


def comm_call(nodes, lists):
    vm = pl.BlockSpec(memory_space=pltpu.VMEM)
    return pl.pallas_call(
        comm_kernel,
        out_shape=(
            jax.ShapeDtypeStruct((512, 512), BF),
            jax.ShapeDtypeStruct((128, 32, 128), BF),
            jax.ShapeDtypeStruct((128, 32, 128), BF),
            jax.ShapeDtypeStruct((128, 16, 128), BF),
        ),
        in_specs=[vm, vm],
        out_specs=(vm,) * 4,
        scratch_shapes=[
            pltpu.VMEM((128, 512), BF),
            pltpu.VMEM((128, 128), F32),
            pltpu.SemaphoreType.DMA((27,)), pltpu.SemaphoreType.DMA((27,)),
            pltpu.SemaphoreType.DMA((12,)), pltpu.SemaphoreType.DMA((12,)),
            pltpu.SemaphoreType.DMA((4,)), pltpu.SemaphoreType.DMA((4,)),
        ],
        compiler_params=pltpu.CompilerParams(
            collective_id=0, has_side_effects=True, vmem_limit_bytes=60 * 2**20),
        cost_estimate=pl.CostEstimate(flops=10**8, bytes_accessed=8 * 10**6, transcendentals=0),
        name="spread",
    )(nodes, lists.reshape(1, -1))


def coarse_call(bufs, cedges, csnd, crcv, w1, b1, w2, b2, gain, shift):
    D = 512
    row = lambda v: v.reshape(1, -1)
    vm = pl.BlockSpec(memory_space=pltpu.VMEM)
    sm = pl.BlockSpec(memory_space=pltpu.SMEM)
    ce = cedges.shape[0]
    return pl.pallas_call(
        coarse_kernel,
        out_shape=(
            jax.ShapeDtypeStruct((ce, D), BF),
            jax.ShapeDtypeStruct((2048, 128), BF),
        ),
        in_specs=[sm, sm] + [vm] * 11,
        out_specs=(vm, vm),
        scratch_shapes=[
            pltpu.VMEM((128 * 80, 128), F32),
            pltpu.VMEM((ce * 4, 128), F32), pltpu.VMEM((ce * 4, 128), F32),
            pltpu.VMEM((2048, 128), F32),
        ],
        compiler_params=pltpu.CompilerParams(vmem_limit_bytes=60 * 2**20),
        cost_estimate=pl.CostEstimate(flops=10**9, bytes_accessed=8 * 10**6, transcendentals=10**5),
        name="coarse",
    )(csnd, crcv, *bufs, cedges, row(crcv), w1, row(b1), w2, row(b2), row(gain), row(shift))


def tail_kernel(node_ref, head, inbound, w1, b1, w2, b2, gain, shift, _, out, wide):
    wide[...] = inbound[...].astype(F32)
    tags = wide[pl.ds(12, 128, stride=16), :].astype(BF)
    total = head[...]
    for s in range(3):
        got = jnp.concatenate([wide[pl.ds(4 * s + j, 128, stride=16), :] for j in range(4)], 1).astype(BF)
        total = total + lax.dot_general(
            tags[:, 32 * s:32 * s + 32], got, (((0,), (0,)), ((), ())), preferred_element_type=F32)
    rows = node_ref[...]
    pre = (
        jnp.dot(rows, w1[0:512, :], preferred_element_type=F32)
        + jnp.dot(total.astype(BF), w1[512:1024, :], preferred_element_type=F32)
        + b1[...]
    )
    y = jnp.dot(silu(pre).astype(BF), w2[...], preferred_element_type=F32) + b2[...]
    out[...] = (rows.astype(F32) + norm_rows(y, gain[...], shift[...])).astype(BF)


def tail_call(nodes, head, inbound, w1, b1, w2, b2, gain, shift, new_nodes):
    D = 512
    row = lambda v: v.reshape(1, D)
    full = lambda s: pl.BlockSpec(s, lambda i: (0,) * len(s))
    return pl.pallas_call(
        tail_kernel,
        out_shape=jax.ShapeDtypeStruct(new_nodes.shape, BF),
        grid=(1,),
        in_specs=[full((32, D)), full((32, D)), full((2048, 128)), full((2 * D, D)), full((1, D)), full((D, D)),
                  full((1, D)), full((1, D)), full((1, D)), pl.BlockSpec(memory_space=pl.ANY)],
        out_specs=full((32, D)),
        scratch_shapes=[pltpu.VMEM((2048, 128), F32)],
        input_output_aliases={9: 0},
        compiler_params=pltpu.CompilerParams(vmem_limit_bytes=48 * 2**20),
        cost_estimate=pl.CostEstimate(flops=10**8, bytes_accessed=3 * 10**6, transcendentals=10**4),
        name="tail",
    )(nodes, head, inbound, w1, row(b1), w2, row(b2), row(gain), row(shift), new_nodes)


AXES = ("gx", "gy")


def on_device(
    node_feats, edge_feats, senders, receivers, send_lists, coarse_edges, coarse_senders, coarse_receivers,
    edge_w1, edge_b1, edge_w2, edge_b2, edge_gain, edge_shift,
    node_w1, node_b1, node_w2, node_b2, node_gain, node_shift,
):
    halo, *bufs = comm_call(node_feats, send_lists)
    new_coarse, outbound = coarse_call(
        bufs, coarse_edges, coarse_senders, coarse_receivers,
        edge_w1, edge_b1, edge_w2, edge_b2, edge_gain, edge_shift)
    inbound = lax.all_to_all(outbound.reshape(128, 16, 128), AXES, 0, 0, tiled=True).reshape(2048, 128)
    new_edges, new_nodes, head = fine_call(
        senders, receivers, edge_feats, node_feats, halo,
        edge_w1, edge_b1, edge_w2, edge_b2, edge_gain, edge_shift,
        node_w1, node_b1, node_w2, node_b2, node_gain, node_shift)
    new_nodes = tail_call(
        node_feats, head, inbound, node_w1, node_b1, node_w2, node_b2, node_gain, node_shift, new_nodes)
    return new_nodes, new_edges, new_coarse


def solution(mesh):
    rows, flat, rep = P(AXES, None), P(AXES), P()
    return jax.shard_map(
        on_device, mesh=mesh,
        in_specs=(rows, rows, flat, flat, flat, rows, flat, flat) + (rep,) * 12,
        out_specs=(rows, rows, rows), check_vma=False,
    )
```

time: 504 us -> 80.8 us (0.16)
  blocking collectives: 193 us -> 0 us
  local copies, waits for them, and re-layouts: 135 us -> 1.49 us
  matrix products: 90.2 us -> 0 us
  Pallas kernels: 0 us -> 73.5 us
  other arithmetic: 47.1 us -> 0 us
  loops' own time: 15.9 us -> 0 us
  starting transfers between devices: 18 us -> 4.78 us
    all_gather x25 -> x0, blocking collectives: 193 us -> none  [gather_in_order(): pieces = lax.all_gather(pieces, axes[k])]
    dot_general x28 -> x0, matrix products: 90.2 us -> none  [the longest x9 39 us: finish_edge(): jnp.dot(hidden, w_second, preferred_element_type=jnp.float32) + b_second]
    pallas_call x0 -> x4, Pallas kernels: none -> 73.5 us  [the longest x1 32.4 us: fine_call(): pl.pallas_call(functools.partial(fine_kernel, esteps=esteps, nodes=N, **k...]
    dynamic_update_slice x24 -> x0, local copies, waits for them, and re-layouts: 50.1 us -> none  [the longest x8 33.4 us: group_step(): lax.dynamic_update_slice_in_dim(summed, window + partial_sum, row_start, 0)]
    gather x19 -> x0, local copies, waits for them, and re-layouts: 32.4 us -> none  [the longest x16 23.8 us: group_step(): send_rows = node_table[send_ids]]
    broadcast_in_dim x9 -> x0, other arithmetic: 18.5 us -> none  [on_device(): lax.scan(group_step, jnp.zeros((node_count, feat_width), jnp.float32), (e...]
    dynamic_slice x16 -> x0, local copies, waits for them, and re-layouts: 16.8 us -> none  [on_device(): lax.scan(group_step, jnp.zeros((node_count, feat_width), jnp.float32), (e...]
    another operation x1 -> x0, loops' own time: 15.9 us -> none  [on_device(): lax.scan(group_step, jnp.zeros((node_count, feat_width), jnp.float32), (e...]
  transfers between devices with their start and end apart: 5 -> 1, of which waited for: 0 -> 0; matrix products, arithmetic and copies ran while one was open for 51% -> 1% of each run, Pallas kernels for 0% -> 40%
where the time goes in v1:
time: 80.8 us; the launch traced here: 80.6 us
  Pallas kernels  73.5 us (91%)
  starting transfers between devices  4.78 us (6%)
  local copies, waits for them, and re-layouts  1.49 us (2%)
    pallas_call x1, Pallas kernels, fine_call(): pl.pallas_call(functools.partial(fine_kernel, esteps=esteps, nodes=N, **k...  32.4 us
    pallas_call x1, Pallas kernels, comm_call(): pl.pallas_call(comm_kernel, out_shape=(jax.ShapeDtypeStruct((512, 512), B...  29.8 us
    pallas_call x1, Pallas kernels, coarse_call(): pl.pallas_call(coarse_kernel, out_shape=(jax.ShapeDtypeStruct((ce, D), BF...  9.65 us
    all_to_all x1, starting transfers between devices, on_device(): lax.all_to_all(outbound.reshape(128, 16, 128), AXES, 0, 0, tiled=True)  4.78 us
    pallas_call x1, Pallas kernels, tail_call(): pl.pallas_call(tail_kernel, out_shape=jax.ShapeDtypeStruct(new_nodes.shap...  1.66 us
  transfers between devices with their start and end apart: 1, of which 0 were waited for; matrix products, arithmetic and copies ran while one was open for 1% of the time, Pallas kernels for 40%

profile of v1, /device:TPU:1, one launch (start us, length us, event | category | flops | bytes accessed | tf_op | source)
XLA Modules:
  0.0 80.6 jit_solution(18054551081091326292)
XLA Ops:
  0.6 29.8 %spread.1 = (bf16[512,512]{1,0:T(8,128)(2,1)}, bf16[128,32,128]{2,1,0:T(8,128)(2,1)}, bf16[128,32,128]{2,1,0:T(8,128)(2,1)}, bf16[128,16,128]{2,1,0:T(8,128)(2,1)}) custom-call(bf16[1280,512]{1,0:T(8,128)(2,1)} %node_ref.5, s32[1,128]{1,0:T(1,128)} %bitcast.31), custom_call_target="tpu_custom_call" | custom-call | flops 100000000 | bytes 8000000 | tf_op jit(solution)/shard_map/spread/pallas_call | solution.py:326
  30.5 0.0 copy-start.8
  30.5 9.6 %coarse.1 = (bf16[160,512]{1,0:T(8,128)(2,1)}, bf16[2048,128]{1,0:T(8,128)(2,1)}) custom-call(s32[160]{0:T(256)} %csnd.1, s32[160]{0:T(256)} %crcv.1, bf16[128,32,128]{2,1,0:T(8,128)(2,1)} %get-tuple-element.14.buf0, bf16[128,32,128]{2,1,0:T(8,128)(2,1)} %get-tuple-element.15.buf1, bf16[128,16,128]{2,1,0:T(8,128)(2,1)} %get-tuple-element.16.buf2, ...), custom_call_target="tpu_custom_call" | custom-call | flops 1000000000 | bytes 8000000 | tf_op jit(solution)/shard_map/coarse/pallas_call | solution.py:356
  40.1 4.8 %all-to-all-start = ((bf16[128,16,128]{2,1,0:T(8,128)(2,1)}), bf16[128,16,128]{2,1,0:T(8,128)(2,1)S(1)}, u32[]{:S(2)}, u32[]{:S(2)}) async-start(bf16[128,16,128]{2,1,0:T(8,128)(2,1)} %bitcast.21), calls=%async_computation | async-start | bytes 1048576 | tf_op jit(solution)/shard_map/all_to_all | solution.py:424
  44.9 0.0 copy-done.8
  44.9 0.6 reshape.54.rcol_a
  45.5 0.0 copy-start
  45.5 0.0 copy-start.1
  45.5 0.0 copy-start.2
  45.5 0.0 copy-start.4
  45.5 0.0 copy-start.5
  45.6 0.0 copy-start.6
  45.6 0.0 copy-start.7
  45.6 32.4 %fine.1 = (bf16[4096,512]{1,0:T(8,128)(2,1)}, bf16[1280,512]{1,0:T(8,128)(2,1)}, f32[32,512]{1,0:T(8,128)}) custom-call(s32[4096]{0:T(1024)} %snd.1, s32[4096]{0:T(1024)} %rcv.1, bf16[4096,512]{1,0:T(8,128)(2,1)} %edges.1, bf16[1280,512]{1,0:T(8,128)(2,1)} %node_ref.5, bf16[512,512]{1,0:T(8,128)(2,1)} %get-tuple-element.12.halo_ref, ...), custom_call_target="tpu_custom_call" | custom-call | flops 10000000000 | bytes 14000000 | tf_op jit(solution)/shard_map/fine/pallas_call | solution.py:117
  78.0 0.0 all-to-all-done
  78.0 0.0 copy-done
  78.0 0.0 copy-done.1
  78.0 0.0 copy-done.2
  78.0 0.0 copy-done.4
  78.0 0.0 copy-done.5
  78.1 0.0 copy-done.6
  78.1 0.0 copy-done.7
  78.1 0.0 copy-start.3
  78.1 0.8 %copy-done.3 = f32[32,512]{1,0:T(8,128)S(1)} copy-done((f32[32,512]{1,0:T(8,128)S(1)}, f32[32,512]{1,0:T(8,128)}, u32[]{:S(2)}) %copy-start.3) | copy-done | bytes 65560
  78.9 1.7 %tail.1 = bf16[1280,512]{1,0:T(8,128)(2,1)} custom-call(bf16[1280,512]{1,0:T(8,128)(2,1)S(1)} %copy-done, f32[32,512]{1,0:T(8,128)S(1)} %copy-done.3, bf16[2048,128]{1,0:T(8,128)(2,1)S(1)} %bitcast.12, bf16[1024,512]{1,0:T(8,128)(2,1)S(1)} %copy-done.1, f32[1,512]{1,0:T(1,128)S(1)} %bitcast.14, ...), custom_call_target="tpu_custom_call", output_to_operand_aliasing={{}: (9, {})} | custom-call | flops 100000000 | bytes 3000000 | tf_op jit(solution)/shard_map/tail/pallas_call | solution.py:397
Async XLA Ops:
  30.5 14.5 %copy-start.8 = (s32[4096]{0:T(1024)S(1)}, s32[4096]{0:T(1024)}, u32[]{:S(2)}) copy-start(s32[4096]{0:T(1024)} %rcv.1) | copy-start | bytes 49156
  40.1 37.9 %all-to-all-start = ((bf16[128,16,128]{2,1,0:T(8,128)(2,1)}), bf16[128,16,128]{2,1,0:T(8,128)(2,1)S(1)}, u32[]{:S(2)}, u32[]{:S(2)}) async-start(bf16[128,16,128]{2,1,0:T(8,128)(2,1)} %bitcast.21), calls=%async_computation | async-start | bytes 1048576 | tf_op jit(solution)/shard_map/all_to_all | solution.py:424
  45.5 32.5 %copy-start = (bf16[1280,512]{1,0:T(8,128)(2,1)S(1)}, bf16[1280,512]{1,0:T(8,128)(2,1)}, u32[]{:S(2)}) copy-start(bf16[1280,512]{1,0:T(8,128)(2,1)} %node_ref.5) | copy-start | bytes 3932164
  45.5 32.5 %copy-start.1 = (bf16[1024,512]{1,0:T(8,128)(2,1)S(1)}, bf16[1024,512]{1,0:T(8,128)(2,1)}, u32[]{:S(2)}) copy-start(bf16[1024,512]{1,0:T(8,128)(2,1)} %w1.5) | copy-start | bytes 3145732
  45.5 32.5 %copy-start.2 = (bf16[512,512]{1,0:T(8,128)(2,1)S(1)}, bf16[512,512]{1,0:T(8,128)(2,1)}, u32[]{:S(2)}) copy-start(bf16[512,512]{1,0:T(8,128)(2,1)} %w2.5) | copy-start | bytes 1572868
  45.5 32.5 %copy-start.4 = (f32[512]{0:T(512)S(1)}, f32[512]{0:T(512)}, u32[]{:S(2)}) copy-start(f32[512]{0:T(512)} %param.35) | copy-start | bytes 6148
  45.5 32.5 %copy-start.5 = (f32[512]{0:T(512)S(1)}, f32[512]{0:T(512)}, u32[]{:S(2)}) copy-start(f32[512]{0:T(512)} %param.37) | copy-start | bytes 6148
  45.6 32.5 %copy-start.6 = (f32[512]{0:T(512)S(1)}, f32[512]{0:T(512)}, u32[]{:S(2)}) copy-start(f32[512]{0:T(512)} %param.38) | copy-start | bytes 6148
  45.6 32.5 %copy-start.7 = (f32[512]{0:T(512)S(1)}, f32[512]{0:T(512)}, u32[]{:S(2)}) copy-start(f32[512]{0:T(512)} %param.39) | copy-start | bytes 6148
  78.1 0.8 %copy-start.3 = (f32[32,512]{1,0:T(8,128)S(1)}, f32[32,512]{1,0:T(8,128)}, u32[]{:S(2)}) copy-start(f32[32,512]{1,0:T(8,128)} %get-tuple-element.13.head) | copy-start | bytes 196612

commit v2 on v1

--- a/solution.py
+++ b/solution.py
@@ -168,10 +168,11 @@
 
 
 def comm_kernel(
-    node_ref, lists,
-    halo, buf0, buf1, buf2,
-    bound, head32,
-    send_sem, recv_sem, csend_sem, crecv_sem, hsend_sem, hrecv_sem,
+    csnd, crcv,
+    node_ref, lists, cedges, crow, w1, b1, w2, b2, gain, shift,
+    halo, new_coarse, outbound,
+    buf0, buf1, buf2, table, rows_s, rows_r, wide, bound, head32,
+    send_sem, recv_sem, hsend_sem, hrecv_sem,
 ):
     a, b = lax.axis_index("gx"), lax.axis_index("gy")
     me = coords(a, b)
@@ -210,24 +211,14 @@
 
     pl.semaphore_wait(barrier, len(partners))
 
-    def hop(p, stage, step):
-        o = ORDERS[p]
-        size = 4 ** stage
-        first = slot(p) // size * size
+    def block(p, step):
+        return (core * 4 + lax.rem(me[ORDERS[p][2]] + 4 - step, 4)) * 16
+
+    def send(p, first, size, to, k):
         part = bufs[p].at[pl.ds(first, size)]
-        k = (p * 3 + stage) * 3 + step - 1
         return pltpu.make_async_remote_copy(
-            src_ref=part, dst_ref=part, send_sem=send_sem.at[k], recv_sem=recv_sem.at[k],
-            device_id=peer(o[stage], step), device_id_type=MESH)
-
-    def across(p, step):
-        o = ORDERS[p]
-        first = (core * 4 + lax.rem(me[o[2]] + 4 - step, 4)) * 16
-        part = bufs[p].at[pl.ds(first, 16)]
-        k = p * 4 + step
-        return pltpu.make_async_remote_copy(
-            src_ref=part, dst_ref=part, send_sem=csend_sem.at[k], recv_sem=crecv_sem.at[k],
-            device_id=sibling, device_id_type=MESH)
+            src_ref=part, dst_ref=part, send_sem=send_sem.at[p, k], recv_sem=recv_sem.at[p, k],
+            device_id=to, device_id_type=MESH)
 
     started = []
 
@@ -236,43 +227,49 @@
         started.append(copy)
         return copy
 
-    stage = [[go(hop(p, 0, s)) for s in (2, 1, 3)] for p in range(3)]
+    def spread(p, stage):
+        size = 4 ** stage
+        first = slot(p) // size * size
+        return [go(send(p, first, size, peer(ORDERS[p][stage], s), 3 * stage + s - 1)) for s in (2, 1, 3)]
+
+    def across(p, first, size, k):
+        return go(send(p, first, size, sibling, k))
+
+    def arrived(copies):
+        for c in copies:
+            c.wait_recv()
+
+    one = [spread(p, 0) for p in range(3)]
     halos = []
     for k, to in enumerate(halo_to):
         halos.append(go(pltpu.make_async_remote_copy(
             src_ref=bound, dst_ref=halo.at[pl.ds(128 * k, 128)], send_sem=hsend_sem.at[k], recv_sem=hrecv_sem.at[k],
             device_id=to, device_id_type=MESH)))
-    nxt = []
+    two = []
     for p in range(3):
-        for c in stage[p]:
-            c.wait_recv()
-        nxt.append([go(hop(p, 1, s)) for s in (2, 1, 3)])
-    stage, nxt, cross = nxt, [], []
+        arrived(one[p])
+        two.append(spread(p, 1))
+    right, left, cross = [], [], []
     for p in range(3):
-        for c in stage[p]:
-            c.wait_recv()
-        nxt.append([go(hop(p, 2, s)) for s in (2, 1, 3)])
-        cross.append(go(across(p, 0)))
-    for i, s in enumerate((2, 1, 3)):
-        for p in range(3):
-            nxt[p][i].wait_recv()
-            cross.append(go(across(p, s)))
-    for c in cross:
-        c.wait_recv()
-
-    for h in halos:
-        h.wait_recv()
-    for k in started:
-        k.wait_send()
-
-
-def coarse_kernel(
-    csnd, crcv,
-    buf0, buf1, buf2, cedges, crow, w1, b1, w2, b2, gain, shift,
-    new_coarse, outbound,
-    table, rows_s, rows_r, wide,
-):
-    bufs = (buf0, buf1, buf2)
+        arrived(two[p])
+        ax = ORDERS[p][2]
+        right.append(go(send(p, block(p, 0), 16, peer(ax, 1), 6)))
+        left.append(go(send(p, block(p, 0), 16, peer(ax, 3), 7)))
+    for p in range(3):
+        cross.append(across(p, block(p, 0), 16, 10))
+    far = []
+    for p in range(3):
+        ax = ORDERS[p][2]
+        right[p].wait_recv()
+        far.append(go(send(p, block(p, 1), 8, peer(ax, 1), 8)))
+        left[p].wait_recv()
+        far.append(go(send(p, block(p, 3) + 8, 8, peer(ax, 3), 9)))
+        cross.append(across(p, block(p, 1), 16, 11))
+        cross.append(across(p, block(p, 3), 16, 12))
+    for p in range(3):
+        arrived(far[2 * p:2 * p + 2])
+        cross.append(across(p, block(p, 2), 16, 13))
+    arrived(cross)
 
     @pl.loop(0, 128)
     def _(q):
@@ -280,13 +277,12 @@
         for p, (r0, n) in enumerate(PIECES):
             pos = {ORDERS[p][2]: u, ORDERS[p][1]: v, ORDERS[p][0]: w}
             aa, bb = device_at(c, pos[1], pos[2], pos[3])
-            at = pl.multiple_of((aa * 32 + bb) * 80 + r0, 8)
-            table[pl.ds(at, n), :] = bufs[p][q].astype(F32)
+            table[pl.ds((aa * 32 + bb) * NCD + r0 // 4, n // 4)] = bufs[p][q].astype(F32).reshape(n // 4, 4, 128)
 
     ce = cedges.shape[0]
     for e in range(ce):
-        rows_s[pl.ds(4 * e, 4), :] = table[pl.ds(pl.multiple_of(csnd[e] * 4, 4), 4), :]
-        rows_r[pl.ds(4 * e, 4), :] = table[pl.ds(pl.multiple_of(crcv[e] * 4, 4), 4), :]
+        rows_s[pl.ds(4 * e, 4), :] = table[csnd[e]]
+        rows_r[pl.ds(4 * e, 4), :] = table[crcv[e]]
     x = cedges[...]
     take = lambda ref: jnp.concatenate([ref[pl.ds(j, ce, stride=4), :] for j in range(4)], 1).astype(BF)
     pre = (
@@ -320,56 +316,42 @@
         wide[pl.ds(12 + j, 128, stride=16), :] = jnp.zeros((128, 128), F32)
     outbound[...] = wide[...].astype(BF)
 
-
-def comm_call(nodes, lists):
-    vm = pl.BlockSpec(memory_space=pltpu.VMEM)
-    return pl.pallas_call(
-        comm_kernel,
-        out_shape=(
-            jax.ShapeDtypeStruct((512, 512), BF),
-            jax.ShapeDtypeStruct((128, 32, 128), BF),
-            jax.ShapeDtypeStruct((128, 32, 128), BF),
-            jax.ShapeDtypeStruct((128, 16, 128), BF),
-        ),
-        in_specs=[vm, vm],
-        out_specs=(vm,) * 4,
-        scratch_shapes=[
-            pltpu.VMEM((128, 512), BF),
-            pltpu.VMEM((128, 128), F32),
-            pltpu.SemaphoreType.DMA((27,)), pltpu.SemaphoreType.DMA((27,)),
-            pltpu.SemaphoreType.DMA((12,)), pltpu.SemaphoreType.DMA((12,)),
-            pltpu.SemaphoreType.DMA((4,)), pltpu.SemaphoreType.DMA((4,)),
-        ],
-        compiler_params=pltpu.CompilerParams(
-            collective_id=0, has_side_effects=True, vmem_limit_bytes=60 * 2**20),
-        cost_estimate=pl.CostEstimate(flops=10**8, bytes_accessed=8 * 10**6, transcendentals=0),
-        name="spread",
-    )(nodes, lists.reshape(1, -1))
-
-
-def coarse_call(bufs, cedges, csnd, crcv, w1, b1, w2, b2, gain, shift):
+    for h in halos:
+        h.wait_recv()
+    for k in started:
+        k.wait_send()
+
+
+def comm_call(nodes, lists, cedges, csnd, crcv, w1, b1, w2, b2, gain, shift):
     D = 512
     row = lambda v: v.reshape(1, -1)
     vm = pl.BlockSpec(memory_space=pltpu.VMEM)
     sm = pl.BlockSpec(memory_space=pltpu.SMEM)
     ce = cedges.shape[0]
     return pl.pallas_call(
-        coarse_kernel,
+        comm_kernel,
         out_shape=(
+            jax.ShapeDtypeStruct((512, D), BF),
             jax.ShapeDtypeStruct((ce, D), BF),
             jax.ShapeDtypeStruct((2048, 128), BF),
         ),
-        in_specs=[sm, sm] + [vm] * 11,
-        out_specs=(vm, vm),
+        in_specs=[sm, sm] + [vm] * 10,
+        out_specs=(vm, vm, vm),
         scratch_shapes=[
-            pltpu.VMEM((128 * 80, 128), F32),
+            pltpu.VMEM((128, 32, 128), BF), pltpu.VMEM((128, 32, 128), BF), pltpu.VMEM((128, 16, 128), BF),
+            pltpu.VMEM((128 * NCD, 4, 128), F32),
             pltpu.VMEM((ce * 4, 128), F32), pltpu.VMEM((ce * 4, 128), F32),
             pltpu.VMEM((2048, 128), F32),
+            pltpu.VMEM((128, D), BF),
+            pltpu.VMEM((128, 128), F32),
+            pltpu.SemaphoreType.DMA((3, 14)), pltpu.SemaphoreType.DMA((3, 14)),
+            pltpu.SemaphoreType.DMA((4,)), pltpu.SemaphoreType.DMA((4,)),
         ],
-        compiler_params=pltpu.CompilerParams(vmem_limit_bytes=60 * 2**20),
+        compiler_params=pltpu.CompilerParams(
+            collective_id=0, has_side_effects=True, vmem_limit_bytes=60 * 2**20),
         cost_estimate=pl.CostEstimate(flops=10**9, bytes_accessed=8 * 10**6, transcendentals=10**5),
         name="coarse",
-    )(csnd, crcv, *bufs, cedges, row(crcv), w1, row(b1), w2, row(b2), row(gain), row(shift))
+    )(csnd, crcv, nodes, row(lists), cedges, row(crcv), w1, row(b1), w2, row(b2), row(gain), row(shift))
 
 
 def tail_kernel(node_ref, head, inbound, w1, b1, w2, b2, gain, shift, _, out, wide):
@@ -417,9 +399,8 @@
     edge_w1, edge_b1, edge_w2, edge_b2, edge_gain, edge_shift,
     node_w1, node_b1, node_w2, node_b2, node_gain, node_shift,
 ):
-    halo, *bufs = comm_call(node_feats, send_lists)
-    new_coarse, outbound = coarse_call(
-        bufs, coarse_edges, coarse_senders, coarse_receivers,
+    halo, new_coarse, outbound = comm_call(
+        node_feats, send_lists, coarse_edges, coarse_senders, coarse_receivers,
         edge_w1, edge_b1, edge_w2, edge_b2, edge_gain, edge_shift)
     inbound = lax.all_to_all(outbound.reshape(128, 16, 128), AXES, 0, 0, tiled=True).reshape(2048, 128)
     new_edges, new_nodes, head = fine_call(

time: 80.8 us -> 81.3 us (level)
  Pallas kernels: 73.5 us -> 72.1 us
  starting transfers between devices: 4.78 us -> 6.04 us
    pallas_call x2 -> x1, Pallas kernels: 39.5 us -> 38.1 us  [comm_call(): pl.pallas_call(comm_kernel, out_shape=(jax.ShapeDtypeStruct((512, D), BF)...]
    all_to_all x1, starting transfers between devices: 4.78 us -> 6.04 us  [on_device(): lax.all_to_all(outbound.reshape(128, 16, 128), AXES, 0, 0, tiled=True)]
where the time goes in v2:
time: 81.3 us; the launch traced here: 81.1 us
  Pallas kernels  72.1 us (89%)
  starting transfers between devices  6.04 us (7%)
  local copies, waits for them, and re-layouts  2.16 us (3%)
    pallas_call x1, Pallas kernels, comm_call(): pl.pallas_call(comm_kernel, out_shape=(jax.ShapeDtypeStruct((512, D), BF)...  38.1 us
    pallas_call x1, Pallas kernels, fine_call(): pl.pallas_call(functools.partial(fine_kernel, esteps=esteps, nodes=N, **k...  32.4 us
    all_to_all x1, starting transfers between devices, on_device(): lax.all_to_all(outbound.reshape(128, 16, 128), AXES, 0, 0, tiled=True)  6.04 us
    pallas_call x1, Pallas kernels, tail_call(): pl.pallas_call(tail_kernel, out_shape=jax.ShapeDtypeStruct(new_nodes.shap...  1.66 us
  transfers between devices with their start and end apart: 1, of which 0 were waited for; matrix products, arithmetic and copies ran while one was open for 1% of the time, Pallas kernels for 40%

profile of v2, /device:TPU:1, one launch (start us, length us, event | category | flops | bytes accessed | tf_op | source)
XLA Modules:
  0.0 81.1 jit_solution(6548797078952972006)
XLA Ops:
  0.6 0.0 copy-start.9
  0.6 38.1 %coarse.1 = (bf16[512,512]{1,0:T(8,128)(2,1)}, bf16[160,512]{1,0:T(8,128)(2,1)}, bf16[2048,128]{1,0:T(8,128)(2,1)}) custom-call(s32[160]{0:T(256)} %csnd.1, s32[160]{0:T(256)} %crcv.1, bf16[1280,512]{1,0:T(8,128)(2,1)} %node_ref.5, s32[1,128]{1,0:T(1,128)} %bitcast.31, bf16[160,512]{1,0:T(8,128)(2,1)} %cedges.1, s32[1,160]{1,0:T(1,128)} %bitcast.30, ...), custom_call_target="tpu_custom_call" | custom-call | flops 1000000000 | bytes 8000000 | tf_op jit(solution)/shard_map/coarse/pallas_call | solution.py:331
  38.7 6.0 %all-to-all-start = ((bf16[128,16,128]{2,1,0:T(8,128)(2,1)}), bf16[128,16,128]{2,1,0:T(8,128)(2,1)S(1)}, u32[]{:S(2)}, u32[]{:S(2)}) async-start(bf16[128,16,128]{2,1,0:T(8,128)(2,1)} %bitcast.21), calls=%async_computation | async-start | bytes 1048576 | tf_op jit(solution)/shard_map/all_to_all | solution.py:405
  44.8 0.0 copy-done.9
  44.8 0.6 reshape.59.rcol_a
  45.4 0.0 copy-start
  45.4 0.0 copy-start.1
  45.4 0.0 copy-start.2
  45.4 0.0 copy-start.4
  45.4 0.0 copy-start.5
  45.4 0.0 copy-start.6
  45.4 0.0 copy-start.7
  45.4 32.4 %fine.1 = (bf16[4096,512]{1,0:T(8,128)(2,1)}, bf16[1280,512]{1,0:T(8,128)(2,1)}, f32[32,512]{1,0:T(8,128)}) custom-call(s32[4096]{0:T(1024)} %snd.1, s32[4096]{0:T(1024)} %rcv.1, bf16[4096,512]{1,0:T(8,128)(2,1)} %edges.1, bf16[1280,512]{1,0:T(8,128)(2,1)} %node_ref.5, bf16[512,512]{1,0:T(8,128)(2,1)} %get-tuple-element.9.halo_ref, ...), custom_call_target="tpu_custom_call" | custom-call | flops 10000000000 | bytes 14000000 | tf_op jit(solution)/shard_map/fine/pallas_call | solution.py:117
  77.8 0.0 all-to-all-done
  77.9 0.0 copy-done
  77.9 0.0 copy-done.1
  77.9 0.0 copy-done.2
  77.9 0.0 copy-done.4
  77.9 0.0 copy-done.5
  77.9 0.0 copy-done.6
  77.9 0.0 copy-done.7
  77.9 0.0 copy-start.3
  77.9 0.8 %copy-done.3 = f32[32,512]{1,0:T(8,128)S(1)} copy-done((f32[32,512]{1,0:T(8,128)S(1)}, f32[32,512]{1,0:T(8,128)}, u32[]{:S(2)}) %copy-start.3) | copy-done | bytes 65560
  78.8 0.0 copy-start.8
  78.8 1.7 %tail.1 = bf16[1280,512]{1,0:T(8,128)(2,1)} custom-call(bf16[1280,512]{1,0:T(8,128)(2,1)S(1)} %copy-done, f32[32,512]{1,0:T(8,128)S(1)} %copy-done.3, bf16[2048,128]{1,0:T(8,128)(2,1)S(1)} %bitcast.12, bf16[1024,512]{1,0:T(8,128)(2,1)S(1)} %copy-done.1, f32[1,512]{1,0:T(1,128)S(1)} %bitcast.14, ...), custom_call_target="tpu_custom_call", output_to_operand_aliasing={{}: (9, {})} | custom-call | flops 100000000 | bytes 3000000 | tf_op jit(solution)/shard_map/tail/pallas_call | solution.py:379
  80.4 0.0 copy-done.8
  80.4 0.7 copy.26
Async XLA Ops:
  0.6 44.1 %copy-start.9 = (s32[4096]{0:T(1024)S(1)}, s32[4096]{0:T(1024)}, u32[]{:S(2)}) copy-start(s32[4096]{0:T(1024)} %rcv.1) | copy-start | bytes 49156
  38.7 39.1 %all-to-all-start = ((bf16[128,16,128]{2,1,0:T(8,128)(2,1)}), bf16[128,16,128]{2,1,0:T(8,128)(2,1)S(1)}, u32[]{:S(2)}, u32[]{:S(2)}) async-start(bf16[128,16,128]{2,1,0:T(8,128)(2,1)} %bitcast.21), calls=%async_computation | async-start | bytes 1048576 | tf_op jit(solution)/shard_map/all_to_all | solution.py:405
  45.4 32.5 %copy-start = (bf16[1280,512]{1,0:T(8,128)(2,1)S(1)}, bf16[1280,512]{1,0:T(8,128)(2,1)}, u32[]{:S(2)}) copy-start(bf16[1280,512]{1,0:T(8,128)(2,1)} %node_ref.5) | copy-start | bytes 3932164
  45.4 32.5 %copy-start.1 = (bf16[1024,512]{1,0:T(8,128)(2,1)S(1)}, bf16[1024,512]{1,0:T(8,128)(2,1)}, u32[]{:S(2)}) copy-start(bf16[1024,512]{1,0:T(8,128)(2,1)} %w1.5) | copy-start | bytes 3145732
  45.4 32.5 %copy-start.2 = (bf16[512,512]{1,0:T(8,128)(2,1)S(1)}, bf16[512,512]{1,0:T(8,128)(2,1)}, u32[]{:S(2)}) copy-start(bf16[512,512]{1,0:T(8,128)(2,1)} %w2.5) | copy-start | bytes 1572868
  45.4 32.5 %copy-start.4 = (f32[512]{0:T(512)S(1)}, f32[512]{0:T(512)}, u32[]{:S(2)}) copy-start(f32[512]{0:T(512)} %param.35) | copy-start | bytes 6148
  45.4 32.5 %copy-start.5 = (f32[512]{0:T(512)S(1)}, f32[512]{0:T(512)}, u32[]{:S(2)}) copy-start(f32[512]{0:T(512)} %param.37) | copy-start | bytes 6148
  45.4 32.5 %copy-start.6 = (f32[512]{0:T(512)S(1)}, f32[512]{0:T(512)}, u32[]{:S(2)}) copy-start(f32[512]{0:T(512)} %param.38) | copy-start | bytes 6148
  45.4 32.5 %copy-start.7 = (f32[512]{0:T(512)S(1)}, f32[512]{0:T(512)}, u32[]{:S(2)}) copy-start(f32[512]{0:T(512)} %param.39) | copy-start | bytes 6148
  77.9 0.8 %copy-start.3 = (f32[32,512]{1,0:T(8,128)S(1)}, f32[32,512]{1,0:T(8,128)}, u32[]{:S(2)}) copy-start(f32[32,512]{1,0:T(8,128)} %get-tuple-element.10.head) | copy-start | bytes 196612
  78.8 1.7 %copy-start.8 = (bf16[160,512]{1,0:T(8,128)(2,1)S(1)}, bf16[160,512]{1,0:T(8,128)(2,1)}, u32[]{:S(2)}) copy-start(bf16[160,512]{1,0:T(8,128)(2,1)} %get-tuple-element.20) | copy-start | bytes 491524

commit v3 on v2

v3 whole, which is shorter than its diff:
```python
import functools
import jax
import jax.numpy as jnp
from jax import lax
from jax.experimental import pallas as pl
from jax.experimental.pallas import tpu as pltpu
from jax.sharding import PartitionSpec as P

BF, F32 = jnp.bfloat16, jnp.float32
MESH = pl.DeviceIdType.MESH
D = 512
NCD = 20
BLK = 256
WIN = 264
PIECES = ((0, 32), (32, 32), (64, 16))
ORDERS = ((3, 2, 1), (2, 1, 3), (1, 3, 2))
SEGMENTS = ((0, 1), (1, 2), (2, 3), (3, 4), (4, 8))


def norm_rows(x, gain, shift):
    mean = jnp.mean(x, -1, keepdims=True)
    c = x - mean
    var = jnp.mean(c * c, -1, keepdims=True)
    return c * lax.rsqrt(var + 1e-05) * gain + shift


def silu(x):
    t = 0.5 * x
    return t + t * jnp.tanh(t)


def iota(shape, dim):
    return lax.broadcasted_iota(jnp.int32, shape, dim)


def coords(a, b):
    return lax.rem(a, 2), (a // 2) * 2 + b // 16, lax.rem(b // 4, 4), lax.rem(b, 4)


def device_at(core, z, x, y):
    return ((z // 2) * 2 + core, lax.rem(z, 2) * 16 + x * 4 + y)


def edge_kernel(
    snd, rcv, csnd, crcv,
    node_ref, lists, edges_in, cedges, crow, w1, b1, w2, b2, gain, shift,
    edges_out, msg_out, new_coarse, inbound,
    edges, new_edges, msg, p_snd, p_rcv, g_a, g_b,
    buf0, buf1, buf2, table, rows_s, rows_r, wide, outb, bound, halo, head32,
    send_sem, recv_sem, hsend_sem, hrecv_sem, out_send, in_recv, load_sem, store_sem,
):
    a, b = lax.axis_index("gx"), lax.axis_index("gy")
    me = coords(a, b)
    core = me[0]
    bufs = (buf0, buf1, buf2)
    nodes = node_ref.shape[0]

    load = pltpu.make_async_copy(edges_in, edges, load_sem)
    load.start()

    def peer(axis, step):
        c = list(me)
        c[axis] = lax.rem(c[axis] + step, 4)
        return device_at(*c)

    sibling = (a + 1 - 2 * core, b)
    halo_to = (
        (lax.rem(a + 1, 4), b), (lax.rem(a + 3, 4), b),
        (a, lax.rem(b + 1, 32)), (a, lax.rem(b + 31, 32)),
    )
    partners = [peer(axis, s) for axis in (1, 2, 3) for s in (1, 2, 3)] + [sibling] + list(halo_to)
    barrier = pltpu.get_barrier_semaphore()
    for p in partners:
        pl.semaphore_signal(barrier, inc=1, device_id=p, device_id_type=MESH)

    own = node_ref[0:32, :].astype(F32)
    for j in range(4):
        head32[pl.ds(j, 32, stride=4), :] = own[:, 128 * j:128 * (j + 1)]

    def slot(p):
        o = ORDERS[p]
        return ((core * 4 + me[o[2]]) * 4 + me[o[1]]) * 4 + me[o[0]]

    for p, (r0, n) in enumerate(PIECES):
        bufs[p][slot(p)] = head32[r0:r0 + n, :].astype(BF)

    hot = (iota((nodes, 128), 0) == lists[...]).astype(F32).astype(BF)
    bound[...] = lax.dot_general(
        hot, node_ref[...], (((0,), (0,)), ((), ())), preferred_element_type=F32).astype(BF)

    def block(p, step):
        return (core * 4 + lax.rem(me[ORDERS[p][2]] + 4 - step, 4)) * 16

    def send(p, first, size, to, k):
        part = bufs[p].at[pl.ds(first, size)]
        return pltpu.make_async_remote_copy(
            src_ref=part, dst_ref=part, send_sem=send_sem.at[p, k], recv_sem=recv_sem.at[p, k],
            device_id=to, device_id_type=MESH)

    started = []

    def go(copy):
        copy.start()
        started.append(copy)
        return copy

    def spread(p, stage):
        size = 4 ** stage
        first = slot(p) // size * size
        return [go(send(p, first, size, peer(ORDERS[p][stage], s), 3 * stage + s - 1)) for s in (2, 1, 3)]

    def across(p, first, size, k):
        return go(send(p, first, size, sibling, k))

    def arrived(copies):
        for c in copies:
            c.wait_recv()

    def project(rows, lo, tab, at, bias):
        n = rows.shape[0]
        v = jnp.dot(rows, w1[lo:lo + 512, :], preferred_element_type=F32)
        if bias is not None:
            v = v + bias
        for j in range(4):
            tab[pl.ds(at, n), j, :] = v[:, 128 * j:128 * (j + 1)]

    def project_own(lo, hi):
        @pl.loop(lo, hi)
        def _(c):
            at = pl.multiple_of(c * 256, 256)
            rows = node_ref[pl.ds(at, 256), :]
            project(rows, 512, p_snd, at, None)
            project(rows, 1024, p_rcv, at, b1[...])

    def gather(k, g):
        base = k * BLK
        for e in range(BLK):
            g[pl.ds(4 * e, 4), :] = p_snd[snd[base + e]] + p_rcv[rcv[base + e]]

    def compute(k, g):
        at = pl.multiple_of(k * BLK, BLK)
        x = edges[pl.ds(at, BLK), :]
        pre = jnp.dot(x, w1[0:512, :], preferred_element_type=F32)
        pre = pre + jnp.concatenate([g[pl.ds(j, BLK, stride=4), :] for j in range(4)], 1)
        y = jnp.dot(silu(pre).astype(BF), w2[...], preferred_element_type=F32) + b2[...]
        m = norm_rows(y, gain[...], shift[...])
        new_edges[pl.ds(at, BLK), :] = (x.astype(F32) + m).astype(BF)
        msg[pl.ds(at, BLK), :] = m.astype(BF)

    last = edges.shape[0] // BLK - 1

    def stores(i):
        part = pl.ds(pl.multiple_of(i * 2 * BLK, 2 * BLK), 2 * BLK)
        return (
            pltpu.make_async_copy(new_edges.at[part], edges_out.at[part], store_sem.at[0, i]),
            pltpu.make_async_copy(msg.at[part], msg_out.at[part], store_sem.at[1, i]),
        )

    def pairs(lo, hi):
        @pl.loop(lo, hi)
        def _(i):
            gather(2 * i + 1, g_b)
            compute(2 * i, g_a)
            gather(jnp.minimum(2 * i + 2, last), g_a)
            compute(2 * i + 1, g_b)
            for c in stores(i):
                c.start()

    project_own(0, nodes // 256)
    pl.semaphore_wait(barrier, len(partners))
    one = [spread(p, 0) for p in range(3)]
    halos = []
    for k, to in enumerate(halo_to):
        halos.append(go(pltpu.make_async_remote_copy(
            src_ref=bound, dst_ref=halo.at[pl.ds(128 * k, 128)], send_sem=hsend_sem.at[k], recv_sem=hrecv_sem.at[k],
            device_id=to, device_id_type=MESH)))
    two = []
    for p in range(3):
        arrived(one[p])
        two.append(spread(p, 1))
    for k in range(4):
        halos[k].wait_recv()
    for k in range(2):
        project(halo[256 * k:256 * (k + 1), :], 512, p_snd, nodes + 256 * k, None)
    load.wait()
    gather(0, g_a)
    pairs(*SEGMENTS[0])
    right, left, cross = [], [], []
    for p in range(3):
        arrived(two[p])
        ax = ORDERS[p][2]
        right.append(go(send(p, block(p, 0), 16, peer(ax, 1), 6)))
        left.append(go(send(p, block(p, 0), 16, peer(ax, 3), 7)))
    for p in range(3):
        cross.append(across(p, block(p, 0), 16, 10))
    pairs(*SEGMENTS[1])
    far = []
    for p in range(3):
        ax = ORDERS[p][2]
        right[p].wait_recv()
        far.append(go(send(p, block(p, 1), 8, peer(ax, 1), 8)))
        left[p].wait_recv()
        far.append(go(send(p, block(p, 3) + 8, 8, peer(ax, 3), 9)))
        cross.append(across(p, block(p, 1), 16, 11))
        cross.append(across(p, block(p, 3), 16, 12))
    pairs(*SEGMENTS[2])
    for p in range(3):
        arrived(far[2 * p:2 * p + 2])
        cross.append(across(p, block(p, 2), 16, 13))
    pairs(*SEGMENTS[3])
    arrived(cross)

    @pl.loop(0, 128)
    def _(q):
        c, u, v, w = q // 64, lax.rem(q // 16, 4), lax.rem(q // 4, 4), lax.rem(q, 4)
        for p, (r0, n) in enumerate(PIECES):
            pos = {ORDERS[p][2]: u, ORDERS[p][1]: v, ORDERS[p][0]: w}
            aa, bb = device_at(c, pos[1], pos[2], pos[3])
            table[pl.ds((aa * 32 + bb) * NCD + r0 // 4, n // 4)] = bufs[p][q].astype(F32).reshape(n // 4, 4, 128)

    ce = cedges.shape[0]
    for e in range(ce):
        rows_s[pl.ds(4 * e, 4), :] = table[csnd[e]]
        rows_r[pl.ds(4 * e, 4), :] = table[crcv[e]]
    x = cedges[...]
    take = lambda ref: jnp.concatenate([ref[pl.ds(j, ce, stride=4), :] for j in range(4)], 1).astype(BF)
    pre = (
        jnp.dot(x, w1[0:512, :], preferred_element_type=F32)
        + jnp.dot(take(rows_s), w1[512:1024, :], preferred_element_type=F32)
        + jnp.dot(take(rows_r), w1[1024:1536, :], preferred_element_type=F32)
        + b1[...]
    )
    y = jnp.dot(silu(pre).astype(BF), w2[...], preferred_element_type=F32) + b2[...]
    m = norm_rows(y, gain[...], shift[...])
    new_coarse[...] = (x.astype(F32) + m).astype(BF)
    mb = m.astype(BF)

    c = crow[...]
    owner = lax.shift_right_logical(c * 52429, 20)
    local = c - owner * NCD
    own_hot = (iota((128, ce), 0) == owner).astype(F32)
    before = (iota((ce, ce), 0) < iota((ce, ce), 1)).astype(F32).astype(BF)
    counts = jnp.dot(own_hot.astype(BF), before, preferred_element_type=F32)
    rank = jnp.sum(own_hot * counts, axis=0, keepdims=True)
    for s in range(3):
        placed = jnp.where(rank == s, own_hot, 0.0).astype(BF)
        got = jnp.dot(placed, mb, preferred_element_type=F32)
        for j in range(4):
            wide[pl.ds(4 * s + j, 128, stride=16), :] = got[:, 128 * j:128 * (j + 1)]
    tags = (iota((128, ce), 0).astype(F32) == rank * 32.0 + local.astype(F32)).astype(F32).astype(BF)
    wide[pl.ds(12, 128, stride=16), :] = lax.dot_general(
        own_hot.astype(BF), tags, (((1,), (1,)), ((), ())), preferred_element_type=F32)
    for j in range(1, 4):
        wide[pl.ds(12 + j, 128, stride=16), :] = jnp.zeros((128, 128), F32)
    outb[...] = wide[...].astype(BF).reshape(128, 16, 128)

    g = a * 32 + b
    inbound[0] = outb[g]

    @pl.loop(1, 128)
    def _(k):
        to = lax.rem(g + k, 128)
        pltpu.make_async_remote_copy(
            src_ref=outb.at[to], dst_ref=inbound.at[k], send_sem=out_send, recv_sem=in_recv,
            device_id=(to // 32, lax.rem(to, 32)), device_id_type=MESH).start()

    pairs(*SEGMENTS[4])

    most = pl.ds(1, 127)
    pltpu.make_async_copy(inbound.at[most], inbound.at[most], in_recv).wait()
    pltpu.make_async_copy(outb.at[most], outb.at[most], out_send).wait()
    for k in started:
        k.wait_send()
    for i in range(edges.shape[0] // (2 * BLK)):
        for c in stores(i):
            c.wait()


def edge_call(snd, rcv, csnd, crcv, nodes, lists, edges, cedges, w1, b1, w2, b2, gain, shift):
    row = lambda v: v.reshape(1, -1)
    vm = pl.BlockSpec(memory_space=pltpu.VMEM)
    sm = pl.BlockSpec(memory_space=pltpu.SMEM)
    hbm = pl.BlockSpec(memory_space=pl.ANY)
    ce, E, N = cedges.shape[0], edges.shape[0], nodes.shape[0]
    return pl.pallas_call(
        edge_kernel,
        out_shape=(
            jax.ShapeDtypeStruct((E, D), BF),
            jax.ShapeDtypeStruct((E, D), BF),
            jax.ShapeDtypeStruct((ce, D), BF),
            jax.ShapeDtypeStruct((128, 16, 128), BF),
        ),
        in_specs=[sm] * 4 + [vm, vm, hbm] + [vm] * 8,
        out_specs=(hbm, hbm, vm, vm),
        scratch_shapes=[
            pltpu.VMEM((E, D), BF), pltpu.VMEM((E, D), BF), pltpu.VMEM((E, D), BF),
            pltpu.VMEM((N + 512, 4, 128), F32), pltpu.VMEM((N, 4, 128), F32),
            pltpu.VMEM((BLK * 4, 128), F32), pltpu.VMEM((BLK * 4, 128), F32),
            pltpu.VMEM((128, 32, 128), BF), pltpu.VMEM((128, 32, 128), BF), pltpu.VMEM((128, 16, 128), BF),
            pltpu.VMEM((128 * NCD, 4, 128), F32),
            pltpu.VMEM((ce * 4, 128), F32), pltpu.VMEM((ce * 4, 128), F32),
            pltpu.VMEM((2048, 128), F32), pltpu.VMEM((128, 16, 128), BF),
            pltpu.VMEM((128, D), BF), pltpu.VMEM((512, D), BF), pltpu.VMEM((128, 128), F32),
            pltpu.SemaphoreType.DMA((3, 14)), pltpu.SemaphoreType.DMA((3, 14)),
            pltpu.SemaphoreType.DMA((4,)), pltpu.SemaphoreType.DMA((4,)),
            pltpu.SemaphoreType.DMA, pltpu.SemaphoreType.DMA,
            pltpu.SemaphoreType.DMA, pltpu.SemaphoreType.DMA((2, 8)),
        ],
        compiler_params=pltpu.CompilerParams(
            collective_id=0, has_side_effects=True, vmem_limit_bytes=60 * 2**20),
        cost_estimate=pl.CostEstimate(flops=7 * 10**9, bytes_accessed=2 * 10**7, transcendentals=2 * 10**6),
        name="edges",
    )(snd, rcv, csnd, crcv, nodes, row(lists), edges, cedges, row(crcv), w1, row(b1), w2, row(b2), row(gain), row(shift))


def node_kernel(
    rcv,
    edges_in, msg, rrow, inbound, node_ref, w1, b1, w2, b2, gain, shift,
    edges_out, new_nodes,
    fsum, wide, copy_sem,
    *, esteps,
):
    i = pl.program_id(0)
    keep = pltpu.make_async_copy(edges_in, edges_out, copy_sem)

    @pl.when(i == 0)
    def _():
        keep.start()
        fsum[...] = jnp.zeros_like(fsum)

    @pl.when(i < esteps)
    def _():
        for k in range(2):
            start = pl.multiple_of((rcv[(2 * i + k) * BLK] // 8) * 8, 8)
            ids = rrow[0, k:k + 1, :]
            hot = (ids - start == iota((WIN, BLK), 0)).astype(F32).astype(BF)
            fsum[pl.ds(start, WIN), :] += jnp.dot(hot, msg[pl.ds(k * BLK, BLK), :], preferred_element_type=F32)

    @pl.when(i == esteps)
    def _():
        wide[...] = inbound[...].astype(F32)
        tags = wide[pl.ds(12, 128, stride=16), :].astype(BF)
        total = fsum[0:32, :]
        for s in range(3):
            got = jnp.concatenate([wide[pl.ds(4 * s + j, 128, stride=16), :] for j in range(4)], 1).astype(BF)
            total = total + lax.dot_general(
                tags[:, 32 * s:32 * s + 32], got, (((0,), (0,)), ((), ())), preferred_element_type=F32)
        fsum[0:32, :] = total

    @pl.when(i >= esteps)
    def _():
        at = pl.multiple_of((i - esteps) * 256, 256)
        rows = node_ref[pl.ds(at, 256), :]
        pre = (
            jnp.dot(rows, w1[0:512, :], preferred_element_type=F32)
            + jnp.dot(fsum[pl.ds(at, 256), :].astype(BF), w1[512:1024, :], preferred_element_type=F32)
            + b1[...]
        )
        y = jnp.dot(silu(pre).astype(BF), w2[...], preferred_element_type=F32) + b2[...]
        new_nodes[...] = (rows.astype(F32) + norm_rows(y, gain[...], shift[...])).astype(BF)

    @pl.when(i == pl.num_programs(0) - 1)
    def _():
        keep.wait()


def node_call(rcv, edges, msg, inbound, nodes, w1, b1, w2, b2, gain, shift):
    E, N = msg.shape[0], nodes.shape[0]
    esteps, nsteps = E // (2 * BLK), N // 256
    row = lambda v: v.reshape(1, D)
    full = lambda s: pl.BlockSpec(s, lambda i, *_: (0,) * len(s))
    hbm = pl.BlockSpec(memory_space=pl.ANY)
    return pl.pallas_call(
        functools.partial(node_kernel, esteps=esteps),
        out_shape=(jax.ShapeDtypeStruct((E, D), BF), jax.ShapeDtypeStruct((N, D), BF)),
        grid_spec=pltpu.PrefetchScalarGridSpec(
            num_scalar_prefetch=1,
            grid=(esteps + nsteps,),
            in_specs=[
                hbm,
                pl.BlockSpec((2 * BLK, D), lambda i, *_: (jnp.minimum(i, esteps - 1), 0)),
                pl.BlockSpec((1, 2, BLK), lambda i, *_: (jnp.minimum(i, esteps - 1), 0, 0)),
                full((2048, 128)), full((N, D)),
                full((2 * D, D)), full((1, D)), full((D, D)), full((1, D)), full((1, D)), full((1, D)),
            ],
            out_specs=(hbm, pl.BlockSpec((256, D), lambda i, *_: (jnp.maximum(i - esteps, 0), 0))),
            scratch_shapes=[
                pltpu.VMEM((N + WIN, D), F32), pltpu.VMEM((2048, 128), F32), pltpu.SemaphoreType.DMA,
            ],
        ),
        compiler_params=pltpu.CompilerParams(vmem_limit_bytes=60 * 2**20, dimension_semantics=("arbitrary",)),
        cost_estimate=pl.CostEstimate(flops=3 * 10**9, bytes_accessed=16 * 10**6, transcendentals=10**6),
        name="nodes",
    )(rcv, edges, msg, rcv.reshape(esteps, 2, BLK), inbound.reshape(2048, 128), nodes,
      w1, row(b1), w2, row(b2), row(gain), row(shift))


AXES = ("gx", "gy")


def on_device(
    node_feats, edge_feats, senders, receivers, send_lists, coarse_edges, coarse_senders, coarse_receivers,
    edge_w1, edge_b1, edge_w2, edge_b2, edge_gain, edge_shift,
    node_w1, node_b1, node_w2, node_b2, node_gain, node_shift,
):
    new_edges, message, new_coarse, inbound = edge_call(
        senders, receivers, coarse_senders, coarse_receivers, node_feats, send_lists, edge_feats, coarse_edges,
        edge_w1, edge_b1, edge_w2, edge_b2, edge_gain, edge_shift)
    new_edges, new_nodes = node_call(
        receivers, new_edges, message, inbound, node_feats,
        node_w1, node_b1, node_w2, node_b2, node_gain, node_shift)
    return new_nodes, new_edges, new_coarse


def solution(mesh):
    rows, flat, rep = P(AXES, None), P(AXES), P()
    return jax.shard_map(
        on_device, mesh=mesh,
        in_specs=(rows, rows, flat, flat, flat, rows, flat, flat) + (rep,) * 12,
        out_specs=(rows, rows, rows), check_vma=False,
    )
```

time: 81.3 us -> 188 us (2.31)
  Pallas kernels: 72.1 us -> 185 us
  starting transfers between devices: 6.04 us -> 0 us
    pallas_call x3 -> x2, Pallas kernels: 72.1 us -> 185 us  [the longest x1 132 us: node_call(): pl.pallas_call(functools.partial(node_kernel, esteps=esteps), out_shape=(...]
    all_to_all x1 -> x0, starting transfers between devices: 6.04 us -> none  [on_device(): lax.all_to_all(outbound.reshape(128, 16, 128), AXES, 0, 0, tiled=True)]
  transfers between devices with their start and end apart: 1 -> 0, of which waited for: 0 -> 0; matrix products, arithmetic and copies ran while one was open for 1% -> 0% of each run, Pallas kernels for 40% -> 0%
where the time goes in v3:
time: 188 us
  Pallas kernels  185 us (98%)
  local copies, waits for them, and re-layouts  2.01 us (1%)
    pallas_call x1, Pallas kernels, node_call(): pl.pallas_call(functools.partial(node_kernel, esteps=esteps), out_shape=(...  132 us
    pallas_call x1, Pallas kernels, edge_call(): pl.pallas_call(edge_kernel, out_shape=(jax.ShapeDtypeStruct((E, D), BF),...  52.7 us

profile of v3, /device:TPU:1, one launch (start us, length us, event | category | flops | bytes accessed | tf_op | source)
XLA Modules:
  0.0 187.5 jit_solution(14254572234348755721)
XLA Ops:
  0.6 1.3 reshape.48.rrow
  2.0 52.7 %edges.1 = (bf16[4096,512]{1,0:T(8,128)(2,1)}, bf16[4096,512]{1,0:T(8,128)(2,1)}, bf16[160,512]{1,0:T(8,128)(2,1)}, bf16[128,16,128]{2,1,0:T(8,128)(2,1)}) custom-call(s32[4096]{0:T(1024)} %snd.1, s32[4096]{0:T(1024)} %rcv.3, s32[160]{0:T(256)} %csnd.1, s32[160]{0:T(256)} %crcv.1, bf16[1280,512]{1,0:T(8,128)(2,1)} %node_ref.3, s32[1,128]{1,0:T(1,128)} %bitcast.21, ...), custom_call_target="tpu_custom_call" | custom-call | flops 7000000000 | bytes 20000000 | tf_op jit(solution)/shard_map/edges/pallas_call | solution.py:285
  54.7 0.0 copy-start
  54.7 132.1 %nodes.1 = (bf16[4096,512]{1,0:T(8,128)(2,1)}, bf16[1280,512]{1,0:T(8,128)(2,1)}) custom-call(s32[4096]{0:T(1024)} %rcv.3, bf16[4096,512]{1,0:T(8,128)(2,1)} %get-tuple-element.9.edges_in, bf16[4096,512]{1,0:T(8,128)(2,1)} %get-tuple-element.10.msg, s32[8,2,256]{2,1,0:T(2,128)} %reshape.48.rrow, bf16[2048,128]{1,0:T(8,128)(2,1)} %bitcast.11, ...), custom_call_target="tpu_custom_call" | custom-call | flops 3000000000 | bytes 16000000 | tf_op jit(solution)/shard_map/nodes/pallas_call | solution.py:373
  186.8 0.0 copy-done
  186.8 0.7 copy.24
Async XLA Ops:
  54.7 132.1 %copy-start = (bf16[160,512]{1,0:T(8,128)(2,1)S(1)}, bf16[160,512]{1,0:T(8,128)(2,1)}, u32[]{:S(2)}) copy-start(bf16[160,512]{1,0:T(8,128)(2,1)} %get-tuple-element.20) | copy-start | bytes 491524

commit v4 on v3

--- a/solution.py
+++ b/solution.py
@@ -14,7 +14,7 @@
 WIN = 264
 PIECES = ((0, 32), (32, 32), (64, 16))
 ORDERS = ((3, 2, 1), (2, 1, 3), (1, 3, 2))
-SEGMENTS = ((0, 1), (1, 2), (2, 3), (3, 4), (4, 8))
+SEGMENTS = ((0, 1), (1, 2), (2, 3), (3, 3), (3, 4), (4, 8))
 
 
 def norm_rows(x, gain, shift):
@@ -166,7 +166,16 @@
             for c in stores(i):
                 c.start()
 
-    project_own(0, nodes // 256)
+    def fill(c):
+        @pl.loop(0, 64)
+        def _(q):
+            u, v, w = q // 16, lax.rem(q // 4, 4), lax.rem(q, 4)
+            for p, (r0, n) in enumerate(PIECES):
+                pos = {ORDERS[p][2]: u, ORDERS[p][1]: v, ORDERS[p][0]: w}
+                aa, bb = device_at(c, pos[1], pos[2], pos[3])
+                table[pl.ds((aa * 32 + bb) * NCD + r0 // 4, n // 4)] = (
+                    bufs[p][c * 64 + q].astype(F32).reshape(n // 4, 4, 128))
+
     pl.semaphore_wait(barrier, len(partners))
     one = [spread(p, 0) for p in range(3)]
     halos = []
@@ -174,6 +183,7 @@
         halos.append(go(pltpu.make_async_remote_copy(
             src_ref=bound, dst_ref=halo.at[pl.ds(128 * k, 128)], send_sem=hsend_sem.at[k], recv_sem=hrecv_sem.at[k],
             device_id=to, device_id_type=MESH)))
+    project_own(0, nodes // 256)
     two = []
     for p in range(3):
         arrived(one[p])
@@ -185,38 +195,23 @@
     load.wait()
     gather(0, g_a)
     pairs(*SEGMENTS[0])
-    right, left, cross = [], [], []
+    three, cross = [], []
     for p in range(3):
         arrived(two[p])
-        ax = ORDERS[p][2]
-        right.append(go(send(p, block(p, 0), 16, peer(ax, 1), 6)))
-        left.append(go(send(p, block(p, 0), 16, peer(ax, 3), 7)))
+        three.append(spread(p, 2))
     for p in range(3):
         cross.append(across(p, block(p, 0), 16, 10))
     pairs(*SEGMENTS[1])
-    far = []
-    for p in range(3):
-        ax = ORDERS[p][2]
-        right[p].wait_recv()
-        far.append(go(send(p, block(p, 1), 8, peer(ax, 1), 8)))
-        left[p].wait_recv()
-        far.append(go(send(p, block(p, 3) + 8, 8, peer(ax, 3), 9)))
-        cross.append(across(p, block(p, 1), 16, 11))
-        cross.append(across(p, block(p, 3), 16, 12))
-    pairs(*SEGMENTS[2])
-    for p in range(3):
-        arrived(far[2 * p:2 * p + 2])
-        cross.append(across(p, block(p, 2), 16, 13))
-    pairs(*SEGMENTS[3])
+    for i, s in enumerate((2, 1, 3)):
+        for p in range(3):
+            three[p][i].wait_recv()
+            cross.append(across(p, block(p, s), 16, 10 + s))
+        if i < 2:
+            pairs(*SEGMENTS[2 + i])
+    fill(core)
+    pairs(*SEGMENTS[4])
     arrived(cross)
-
-    @pl.loop(0, 128)
-    def _(q):
-        c, u, v, w = q // 64, lax.rem(q // 16, 4), lax.rem(q // 4, 4), lax.rem(q, 4)
-        for p, (r0, n) in enumerate(PIECES):
-            pos = {ORDERS[p][2]: u, ORDERS[p][1]: v, ORDERS[p][0]: w}
-            aa, bb = device_at(c, pos[1], pos[2], pos[3])
-            table[pl.ds((aa * 32 + bb) * NCD + r0 // 4, n // 4)] = bufs[p][q].astype(F32).reshape(n // 4, 4, 128)
+    fill(1 - core)
 
     ce = cedges.shape[0]
     for e in range(ce):
@@ -264,7 +259,7 @@
             src_ref=outb.at[to], dst_ref=inbound.at[k], send_sem=out_send, recv_sem=in_recv,
             device_id=(to // 32, lax.rem(to, 32)), device_id_type=MESH).start()
 
-    pairs(*SEGMENTS[4])
+    pairs(*SEGMENTS[5])
 
     most = pl.ds(1, 127)
     pltpu.make_async_copy(inbound.at[most], inbound.at[most], in_recv).wait()
@@ -315,84 +310,85 @@
 
 def node_kernel(
     rcv,
-    edges_in, msg, rrow, inbound, node_ref, w1, b1, w2, b2, gain, shift,
-    edges_out, new_nodes,
-    fsum, wide, copy_sem,
-    *, esteps,
+    rrow, edges_in, msg_in, coarse_in, inbound_in, nodes_in, w1_in, w2_in, b1, b2, gain, shift,
+    edges_out, coarse_out, nodes_out,
+    edges, msg, coarse, inbound, node_ref, w1, w2, new_nodes, fsum, wide,
+    msg_sem, edge_sem, back_sem, small_sem, node_sem,
 ):
-    i = pl.program_id(0)
-    keep = pltpu.make_async_copy(edges_in, edges_out, copy_sem)
-
-    @pl.when(i == 0)
-    def _():
-        keep.start()
-        fsum[...] = jnp.zeros_like(fsum)
-
-    @pl.when(i < esteps)
-    def _():
-        for k in range(2):
-            start = pl.multiple_of((rcv[(2 * i + k) * BLK] // 8) * 8, 8)
-            ids = rrow[0, k:k + 1, :]
+    steps, nsteps = msg.shape[0] // (2 * BLK), node_ref.shape[0] // BLK
+    part = lambda i: pl.ds(2 * BLK * i, 2 * BLK)
+    loads = [pltpu.make_async_copy(msg_in.at[part(i)], msg.at[part(i)], msg_sem.at[i]) for i in range(steps)]
+    small = [
+        pltpu.make_async_copy(src, dst, small_sem.at[k]) for k, (src, dst) in enumerate((
+            (inbound_in, inbound), (nodes_in, node_ref), (w1_in, w1), (w2_in, w2), (coarse_in, coarse)))
+    ]
+    there = [pltpu.make_async_copy(edges_in.at[part(i)], edges.at[part(i)], edge_sem.at[i]) for i in range(steps)]
+    back = [pltpu.make_async_copy(edges.at[part(i)], edges_out.at[part(i)], back_sem.at[i]) for i in range(steps)]
+    back.append(pltpu.make_async_copy(coarse, coarse_out, back_sem.at[steps]))
+    for c in loads + small + there:
+        c.start()
+    fsum[...] = jnp.zeros_like(fsum)
+    for i in range(steps):
+        loads[i].wait()
+        for k in (2 * i, 2 * i + 1):
+            start = pl.multiple_of((rcv[k * BLK] // 8) * 8, 8)
+            ids = rrow[:, k * BLK:(k + 1) * BLK]
             hot = (ids - start == iota((WIN, BLK), 0)).astype(F32).astype(BF)
-            fsum[pl.ds(start, WIN), :] += jnp.dot(hot, msg[pl.ds(k * BLK, BLK), :], preferred_element_type=F32)
-
-    @pl.when(i == esteps)
-    def _():
-        wide[...] = inbound[...].astype(F32)
-        tags = wide[pl.ds(12, 128, stride=16), :].astype(BF)
-        total = fsum[0:32, :]
-        for s in range(3):
-            got = jnp.concatenate([wide[pl.ds(4 * s + j, 128, stride=16), :] for j in range(4)], 1).astype(BF)
-            total = total + lax.dot_general(
-                tags[:, 32 * s:32 * s + 32], got, (((0,), (0,)), ((), ())), preferred_element_type=F32)
-        fsum[0:32, :] = total
-
-    @pl.when(i >= esteps)
-    def _():
-        at = pl.multiple_of((i - esteps) * 256, 256)
-        rows = node_ref[pl.ds(at, 256), :]
+            fsum[pl.ds(start, WIN), :] += jnp.dot(hot, msg[k * BLK:(k + 1) * BLK, :], preferred_element_type=F32)
+    for c in small:
+        c.wait()
+    back[steps].start()
+    for i in range(steps):
+        there[i].wait()
+        back[i].start()
+
+    wide[...] = inbound[...].astype(F32)
+    tags = wide[pl.ds(12, 128, stride=16), :].astype(BF)
+    total = fsum[0:32, :]
+    for s in range(3):
+        got = jnp.concatenate([wide[pl.ds(4 * s + j, 128, stride=16), :] for j in range(4)], 1).astype(BF)
+        total = total + lax.dot_general(
+            tags[:, 32 * s:32 * s + 32], got, (((0,), (0,)), ((), ())), preferred_element_type=F32)
+    fsum[0:32, :] = total
+
+    for c in range(nsteps):
+        at = pl.ds(c * BLK, BLK)
+        rows = node_ref[at, :]
         pre = (
             jnp.dot(rows, w1[0:512, :], preferred_element_type=F32)
-            + jnp.dot(fsum[pl.ds(at, 256), :].astype(BF), w1[512:1024, :], preferred_element_type=F32)
+            + jnp.dot(fsum[at, :].astype(BF), w1[512:1024, :], preferred_element_type=F32)
             + b1[...]
         )
         y = jnp.dot(silu(pre).astype(BF), w2[...], preferred_element_type=F32) + b2[...]
-        new_nodes[...] = (rows.astype(F32) + norm_rows(y, gain[...], shift[...])).astype(BF)
-
-    @pl.when(i == pl.num_programs(0) - 1)
-    def _():
-        keep.wait()
-
-
-def node_call(rcv, edges, msg, inbound, nodes, w1, b1, w2, b2, gain, shift):
+        new_nodes[at, :] = (rows.astype(F32) + norm_rows(y, gain[...], shift[...])).astype(BF)
+        back.append(pltpu.make_async_copy(new_nodes.at[at], nodes_out.at[at], node_sem.at[c]))
+        back[-1].start()
+    for c in back:
+        c.wait()
+
+
+def node_call(rcv, edges, msg, coarse, inbound, nodes, w1, b1, w2, b2, gain, shift):
     E, N = msg.shape[0], nodes.shape[0]
-    esteps, nsteps = E // (2 * BLK), N // 256
-    row = lambda v: v.reshape(1, D)
-    full = lambda s: pl.BlockSpec(s, lambda i, *_: (0,) * len(s))
+    row = lambda v: v.reshape(1, -1)
+    vm = pl.BlockSpec(memory_space=pltpu.VMEM)
+    sm = pl.BlockSpec(memory_space=pltpu.SMEM)
     hbm = pl.BlockSpec(memory_space=pl.ANY)
+    like = lambda v: pltpu.VMEM(v.shape, v.dtype)
+    inbound = inbound.reshape(2048, 128)
     return pl.pallas_call(
-        functools.partial(node_kernel, esteps=esteps),
-        out_shape=(jax.ShapeDtypeStruct((E, D), BF), jax.ShapeDtypeStruct((N, D), BF)),
-        grid_spec=pltpu.PrefetchScalarGridSpec(
-            num_scalar_prefetch=1,
-            grid=(esteps + nsteps,),
-            in_specs=[
-                hbm,
-                pl.BlockSpec((2 * BLK, D), lambda i, *_: (jnp.minimum(i, esteps - 1), 0)),
-                pl.BlockSpec((1, 2, BLK), lambda i, *_: (jnp.minimum(i, esteps - 1), 0, 0)),
-                full((2048, 128)), full((N, D)),
-                full((2 * D, D)), full((1, D)), full((D, D)), full((1, D)), full((1, D)), full((1, D)),
-            ],
-            out_specs=(hbm, pl.BlockSpec((256, D), lambda i, *_: (jnp.maximum(i - esteps, 0), 0))),
-            scratch_shapes=[
-                pltpu.VMEM((N + WIN, D), F32), pltpu.VMEM((2048, 128), F32), pltpu.SemaphoreType.DMA,
-            ],
-        ),
-        compiler_params=pltpu.CompilerParams(vmem_limit_bytes=60 * 2**20, dimension_semantics=("arbitrary",)),
+        node_kernel,
+        out_shape=tuple(jax.ShapeDtypeStruct(v.shape, BF) for v in (edges, coarse, nodes)),
+        in_specs=[sm, vm] + [hbm] * 7 + [vm] * 4,
+        out_specs=(hbm, hbm, hbm),
+        scratch_shapes=[like(v) for v in (edges, msg, coarse, inbound, nodes, w1, w2, nodes)] + [
+            pltpu.VMEM((N + WIN, D), F32), pltpu.VMEM((2048, 128), F32),
+            pltpu.SemaphoreType.DMA((8,)), pltpu.SemaphoreType.DMA((8,)), pltpu.SemaphoreType.DMA((9,)),
+            pltpu.SemaphoreType.DMA((5,)), pltpu.SemaphoreType.DMA((5,)),
+        ],
+        compiler_params=pltpu.CompilerParams(vmem_limit_bytes=60 * 2**20),
         cost_estimate=pl.CostEstimate(flops=3 * 10**9, bytes_accessed=16 * 10**6, transcendentals=10**6),
         name="nodes",
-    )(rcv, edges, msg, rcv.reshape(esteps, 2, BLK), inbound.reshape(2048, 128), nodes,
-      w1, row(b1), w2, row(b2), row(gain), row(shift))
+    )(rcv, row(rcv), edges, msg, coarse, inbound, nodes, w1, w2, row(b1), row(b2), row(gain), row(shift))
 
 
 AXES = ("gx", "gy")
@@ -406,8 +402,8 @@
     new_edges, message, new_coarse, inbound = edge_call(
         senders, receivers, coarse_senders, coarse_receivers, node_feats, send_lists, edge_feats, coarse_edges,
         edge_w1, edge_b1, edge_w2, edge_b2, edge_gain, edge_shift)
-    new_edges, new_nodes = node_call(
-        receivers, new_edges, message, inbound, node_feats,
+    new_edges, new_coarse, new_nodes = node_call(
+        receivers, new_edges, message, new_coarse, inbound, node_feats,
         node_w1, node_b1, node_w2, node_b2, node_gain, node_shift)
     return new_nodes, new_edges, new_coarse
 

time: 188 us -> 60.3 us (0.32)
  Pallas kernels: 185 us -> 58.9 us
  local copies, waits for them, and re-layouts: 2.01 us -> 0 us
    pallas_call x1, Pallas kernels: 132 us -> 10.1 us  [node_call(): pl.pallas_call(node_kernel, out_shape=tuple((jax.ShapeDtypeStruct(v.shape...]
    pallas_call x1, Pallas kernels: 52.7 us -> 48.9 us  [edge_call(): pl.pallas_call(edge_kernel, out_shape=(jax.ShapeDtypeStruct((E, D), BF),...]
where the time goes in v4:
time: 60.3 us; the launch traced here: 59.7 us
  Pallas kernels  58.9 us (98%)
  between operations  0.8 us (1%)
    pallas_call x1, Pallas kernels, edge_call(): pl.pallas_call(edge_kernel, out_shape=(jax.ShapeDtypeStruct((E, D), BF),...  48.9 us
    pallas_call x1, Pallas kernels, node_call(): pl.pallas_call(node_kernel, out_shape=tuple((jax.ShapeDtypeStruct(v.shape...  10.1 us

profile of v4, /device:TPU:1, one launch (start us, length us, event | category | flops | bytes accessed | tf_op | source)
XLA Modules:
  0.0 59.7 jit_solution(18442240598392563832)
XLA Ops:
  0.6 48.9 %edges.1 = (bf16[4096,512]{1,0:T(8,128)(2,1)}, bf16[4096,512]{1,0:T(8,128)(2,1)}, bf16[160,512]{1,0:T(8,128)(2,1)}, bf16[128,16,128]{2,1,0:T(8,128)(2,1)}) custom-call(s32[4096]{0:T(1024)} %snd.1, s32[4096]{0:T(1024)} %rcv.3, s32[160]{0:T(256)} %csnd.1, s32[160]{0:T(256)} %crcv.1, bf16[1280,512]{1,0:T(8,128)(2,1)} %nodes_in.1, s32[1,128]{1,0:T(1,128)} %bitcast.23, ...), custom_call_target="tpu_custom_call" | custom-call | flops 7000000000 | bytes 20000000 | tf_op jit(solution)/shard_map/edges/pallas_call | solution.py:280
  49.5 10.1 %nodes.1 = (bf16[4096,512]{1,0:T(8,128)(2,1)}, bf16[160,512]{1,0:T(8,128)(2,1)}, bf16[1280,512]{1,0:T(8,128)(2,1)}) custom-call(s32[4096]{0:T(1024)} %rcv.3, s32[1,4096]{1,0:T(1,128)} %bitcast.13, bf16[4096,512]{1,0:T(8,128)(2,1)} %get-tuple-element.10.edges_in, bf16[4096,512]{1,0:T(8,128)(2,1)} %get-tuple-element.11.msg_in, ...), custom_call_target="tpu_custom_call" | custom-call | flops 3000000000 | bytes 16000000 | tf_op jit(solution)/shard_map/nodes/pallas_call | solution.py:378

commit v5 on v4

--- a/solution.py
+++ b/solution.py
@@ -14,7 +14,7 @@
 WIN = 264
 PIECES = ((0, 32), (32, 32), (64, 16))
 ORDERS = ((3, 2, 1), (2, 1, 3), (1, 3, 2))
-SEGMENTS = ((0, 1), (1, 2), (2, 3), (3, 3), (3, 4), (4, 8))
+SEGMENTS = ((0, 1), (1, 3), (3, 4), (4, 4), (4, 5), (5, 8))
 
 
 def norm_rows(x, gain, shift):
@@ -43,9 +43,9 @@
 
 def edge_kernel(
     snd, rcv, csnd, crcv,
-    node_ref, lists, edges_in, cedges, crow, w1, b1, w2, b2, gain, shift,
+    nodes_in, lists, edges_in, cedges, crow, w1_in, b1, w2_in, b2, gain, shift,
     edges_out, msg_out, new_coarse, inbound,
-    edges, new_edges, msg, p_snd, p_rcv, g_a, g_b,
+    node_ref, w1, w2, edges, new_edges, msg, p_snd, p_rcv, g_a, g_b,
     buf0, buf1, buf2, table, rows_s, rows_r, wide, outb, bound, halo, head32,
     send_sem, recv_sem, hsend_sem, hrecv_sem, out_send, in_recv, load_sem, store_sem,
 ):
@@ -55,8 +55,12 @@
     bufs = (buf0, buf1, buf2)
     nodes = node_ref.shape[0]
 
-    load = pltpu.make_async_copy(edges_in, edges, load_sem)
-    load.start()
+    loads = [
+        pltpu.make_async_copy(src, dst, load_sem.at[k])
+        for k, (src, dst) in enumerate(((nodes_in, node_ref), (w1_in, w1), (w2_in, w2), (edges_in, edges)))
+    ]
+    for c in loads:
+        c.start()
 
     def peer(axis, step):
         c = list(me)
@@ -73,6 +77,7 @@
     for p in partners:
         pl.semaphore_signal(barrier, inc=1, device_id=p, device_id_type=MESH)
 
+    loads[0].wait()
     own = node_ref[0:32, :].astype(F32)
     for j in range(4):
         head32[pl.ds(j, 32, stride=4), :] = own[:, 128 * j:128 * (j + 1)]
@@ -132,19 +137,24 @@
             project(rows, 512, p_snd, at, None)
             project(rows, 1024, p_rcv, at, b1[...])
 
-    def gather(k, g):
+    def gather(k, g, lo=0, hi=BLK):
         base = k * BLK
-        for e in range(BLK):
+        for e in range(lo, hi):
             g[pl.ds(4 * e, 4), :] = p_snd[snd[base + e]] + p_rcv[rcv[base + e]]
 
-    def compute(k, g):
-        at = pl.multiple_of(k * BLK, BLK)
-        x = edges[pl.ds(at, BLK), :]
+    def first(k, g):
+        x = edges[pl.ds(pl.multiple_of(k * BLK, BLK), BLK), :]
         pre = jnp.dot(x, w1[0:512, :], preferred_element_type=F32)
         pre = pre + jnp.concatenate([g[pl.ds(j, BLK, stride=4), :] for j in range(4)], 1)
-        y = jnp.dot(silu(pre).astype(BF), w2[...], preferred_element_type=F32) + b2[...]
+        return silu(pre).astype(BF)
+
+    def second(h):
+        return jnp.dot(h, w2[...], preferred_element_type=F32) + b2[...]
+
+    def third(k, y):
+        at = pl.multiple_of(k * BLK, BLK)
         m = norm_rows(y, gain[...], shift[...])
-        new_edges[pl.ds(at, BLK), :] = (x.astype(F32) + m).astype(BF)
+        new_edges[pl.ds(at, BLK), :] = (edges[pl.ds(at, BLK), :].astype(F32) + m).astype(BF)
         msg[pl.ds(at, BLK), :] = m.astype(BF)
 
     last = edges.shape[0] // BLK - 1
@@ -159,10 +169,18 @@
     def pairs(lo, hi):
         @pl.loop(lo, hi)
         def _(i):
-            gather(2 * i + 1, g_b)
-            compute(2 * i, g_a)
-            gather(jnp.minimum(2 * i + 2, last), g_a)
-            compute(2 * i + 1, g_b)
+            half = BLK // 2
+            k, n = 2 * i, jnp.minimum(2 * i + 2, last - 1)
+            h_a = first(k, g_a)
+            h_b = first(k + 1, g_b)
+            gather(n, g_a, 0, half)
+            y_a = second(h_a)
+            gather(n, g_a, half, BLK)
+            y_b = second(h_b)
+            gather(n + 1, g_b, 0, half)
+            third(k, y_a)
+            gather(n + 1, g_b, half, BLK)
+            third(k + 1, y_b)
             for c in stores(i):
                 c.start()
 
@@ -183,6 +201,7 @@
         halos.append(go(pltpu.make_async_remote_copy(
             src_ref=bound, dst_ref=halo.at[pl.ds(128 * k, 128)], send_sem=hsend_sem.at[k], recv_sem=hrecv_sem.at[k],
             device_id=to, device_id_type=MESH)))
+    loads[1].wait()
     project_own(0, nodes // 256)
     two = []
     for p in range(3):
@@ -192,8 +211,10 @@
         halos[k].wait_recv()
     for k in range(2):
         project(halo[256 * k:256 * (k + 1), :], 512, p_snd, nodes + 256 * k, None)
-    load.wait()
+    loads[2].wait()
+    loads[3].wait()
     gather(0, g_a)
+    gather(1, g_b)
     pairs(*SEGMENTS[0])
     three, cross = [], []
     for p in range(3):
@@ -285,9 +306,10 @@
             jax.ShapeDtypeStruct((ce, D), BF),
             jax.ShapeDtypeStruct((128, 16, 128), BF),
         ),
-        in_specs=[sm] * 4 + [vm, vm, hbm] + [vm] * 8,
+        in_specs=[sm] * 4 + [hbm, vm, hbm, vm, vm, hbm, vm, hbm] + [vm] * 3,
         out_specs=(hbm, hbm, vm, vm),
         scratch_shapes=[
+            pltpu.VMEM((N, D), BF), pltpu.VMEM((3 * D, D), BF), pltpu.VMEM((D, D), BF),
             pltpu.VMEM((E, D), BF), pltpu.VMEM((E, D), BF), pltpu.VMEM((E, D), BF),
             pltpu.VMEM((N + 512, 4, 128), F32), pltpu.VMEM((N, 4, 128), F32),
             pltpu.VMEM((BLK * 4, 128), F32), pltpu.VMEM((BLK * 4, 128), F32),
@@ -299,7 +321,7 @@
             pltpu.SemaphoreType.DMA((3, 14)), pltpu.SemaphoreType.DMA((3, 14)),
             pltpu.SemaphoreType.DMA((4,)), pltpu.SemaphoreType.DMA((4,)),
             pltpu.SemaphoreType.DMA, pltpu.SemaphoreType.DMA,
-            pltpu.SemaphoreType.DMA, pltpu.SemaphoreType.DMA((2, 8)),
+            pltpu.SemaphoreType.DMA((4,)), pltpu.SemaphoreType.DMA((2, 8)),
         ],
         compiler_params=pltpu.CompilerParams(
             collective_id=0, has_side_effects=True, vmem_limit_bytes=60 * 2**20),
@@ -320,7 +342,7 @@
     loads = [pltpu.make_async_copy(msg_in.at[part(i)], msg.at[part(i)], msg_sem.at[i]) for i in range(steps)]
     small = [
         pltpu.make_async_copy(src, dst, small_sem.at[k]) for k, (src, dst) in enumerate((
-            (inbound_in, inbound), (nodes_in, node_ref), (w1_in, w1), (w2_in, w2), (coarse_in, coarse)))
+            (nodes_in, node_ref), (w1_in, w1), (w2_in, w2), (inbound_in, inbound), (coarse_in, coarse)))
     ]
     there = [pltpu.make_async_copy(edges_in.at[part(i)], edges.at[part(i)], edge_sem.at[i]) for i in range(steps)]
     back = [pltpu.make_async_copy(edges.at[part(i)], edges_out.at[part(i)], back_sem.at[i]) for i in range(steps)]

time: 60.3 us -> 58.1 us (0.964)
  Pallas kernels: 58.9 us -> 57 us
    pallas_call x1, Pallas kernels: 48.9 us -> 47 us  [edge_call(): pl.pallas_call(edge_kernel, out_shape=(jax.ShapeDtypeStruct((E, D), BF),...]
where the time goes in v5:
time: 58.1 us; the launch traced here: 57.8 us
  Pallas kernels  57 us (98%)
  between operations  0.8 us (1%)
    pallas_call x1, Pallas kernels, edge_call(): pl.pallas_call(edge_kernel, out_shape=(jax.ShapeDtypeStruct((E, D), BF),...  47 us
    pallas_call x1, Pallas kernels, node_call(): pl.pallas_call(node_kernel, out_shape=tuple((jax.ShapeDtypeStruct(v.shape...  10.1 us

profile of v5, /device:TPU:1, one launch (start us, length us, event | category | flops | bytes accessed | tf_op | source)
XLA Modules:
  0.0 57.8 jit_solution(5123945526243941474)
XLA Ops:
  0.6 47.0 %edges.1 = (bf16[4096,512]{1,0:T(8,128)(2,1)}, bf16[4096,512]{1,0:T(8,128)(2,1)}, bf16[160,512]{1,0:T(8,128)(2,1)}, bf16[128,16,128]{2,1,0:T(8,128)(2,1)}) custom-call(s32[4096]{0:T(1024)} %snd.1, s32[4096]{0:T(1024)} %rcv.3, s32[160]{0:T(256)} %csnd.1, s32[160]{0:T(256)} %crcv.1, bf16[1280,512]{1,0:T(8,128)(2,1)} %nodes_in.3, s32[1,128]{1,0:T(1,128)} %bitcast.23, ...), custom_call_target="tpu_custom_call" | custom-call | flops 7000000000 | bytes 20000000 | tf_op jit(solution)/shard_map/edges/pallas_call | solution.py:301
  47.6 10.1 %nodes.1 = (bf16[4096,512]{1,0:T(8,128)(2,1)}, bf16[160,512]{1,0:T(8,128)(2,1)}, bf16[1280,512]{1,0:T(8,128)(2,1)}) custom-call(s32[4096]{0:T(1024)} %rcv.3, s32[1,4096]{1,0:T(1,128)} %bitcast.13, bf16[4096,512]{1,0:T(8,128)(2,1)} %get-tuple-element.10.edges_in, bf16[4096,512]{1,0:T(8,128)(2,1)} %get-tuple-element.11.msg_in, ...), custom_call_target="tpu_custom_call" | custom-call | flops 3000000000 | bytes 16000000 | tf_op jit(solution)/shard_map/nodes/pallas_call | solution.py:400

commit v6 on v5

--- a/solution.py
+++ b/solution.py
@@ -44,10 +44,10 @@
 def edge_kernel(
     snd, rcv, csnd, crcv,
     nodes_in, lists, edges_in, cedges, crow, w1_in, b1, w2_in, b2, gain, shift,
-    edges_out, msg_out, new_coarse, inbound,
-    node_ref, w1, w2, edges, new_edges, msg, p_snd, p_rcv, g_a, g_b,
+    new_edges, msg, new_coarse, inbound,
+    node_ref, w1, w2, edges, p_snd, p_rcv, g_a, g_b,
     buf0, buf1, buf2, table, rows_s, rows_r, wide, outb, bound, halo, head32,
-    send_sem, recv_sem, hsend_sem, hrecv_sem, out_send, in_recv, load_sem, store_sem,
+    send_sem, recv_sem, hsend_sem, hrecv_sem, out_send, in_recv, load_sem,
 ):
     a, b = lax.axis_index("gx"), lax.axis_index("gy")
     me = coords(a, b)
@@ -158,13 +158,6 @@
         msg[pl.ds(at, BLK), :] = m.astype(BF)
 
     last = edges.shape[0] // BLK - 1
-
-    def stores(i):
-        part = pl.ds(pl.multiple_of(i * 2 * BLK, 2 * BLK), 2 * BLK)
-        return (
-            pltpu.make_async_copy(new_edges.at[part], edges_out.at[part], store_sem.at[0, i]),
-            pltpu.make_async_copy(msg.at[part], msg_out.at[part], store_sem.at[1, i]),
-        )
 
     def pairs(lo, hi):
         @pl.loop(lo, hi)
@@ -181,8 +174,6 @@
             third(k, y_a)
             gather(n + 1, g_b, half, BLK)
             third(k + 1, y_b)
-            for c in stores(i):
-                c.start()
 
     def fill(c):
         @pl.loop(0, 64)
@@ -287,9 +278,6 @@
     pltpu.make_async_copy(outb.at[most], outb.at[most], out_send).wait()
     for k in started:
         k.wait_send()
-    for i in range(edges.shape[0] // (2 * BLK)):
-        for c in stores(i):
-            c.wait()
 
 
 def edge_call(snd, rcv, csnd, crcv, nodes, lists, edges, cedges, w1, b1, w2, b2, gain, shift):
@@ -301,16 +289,16 @@
     return pl.pallas_call(
         edge_kernel,
         out_shape=(
-            jax.ShapeDtypeStruct((E, D), BF),
-            jax.ShapeDtypeStruct((E, D), BF),
+            pltpu.VMEM((E, D), BF),
+            pltpu.VMEM((E, D), BF),
             jax.ShapeDtypeStruct((ce, D), BF),
             jax.ShapeDtypeStruct((128, 16, 128), BF),
         ),
         in_specs=[sm] * 4 + [hbm, vm, hbm, vm, vm, hbm, vm, hbm] + [vm] * 3,
-        out_specs=(hbm, hbm, vm, vm),
+        out_specs=(vm, vm, vm, vm),
         scratch_shapes=[
             pltpu.VMEM((N, D), BF), pltpu.VMEM((3 * D, D), BF), pltpu.VMEM((D, D), BF),
-            pltpu.VMEM((E, D), BF), pltpu.VMEM((E, D), BF), pltpu.VMEM((E, D), BF),
+            pltpu.VMEM((E, D), BF),
             pltpu.VMEM((N + 512, 4, 128), F32), pltpu.VMEM((N, 4, 128), F32),
             pltpu.VMEM((BLK * 4, 128), F32), pltpu.VMEM((BLK * 4, 128), F32),
             pltpu.VMEM((128, 32, 128), BF), pltpu.VMEM((128, 32, 128), BF), pltpu.VMEM((128, 16, 128), BF),
@@ -321,49 +309,50 @@
             pltpu.SemaphoreType.DMA((3, 14)), pltpu.SemaphoreType.DMA((3, 14)),
             pltpu.SemaphoreType.DMA((4,)), pltpu.SemaphoreType.DMA((4,)),
             pltpu.SemaphoreType.DMA, pltpu.SemaphoreType.DMA,
-            pltpu.SemaphoreType.DMA((4,)), pltpu.SemaphoreType.DMA((2, 8)),
+            pltpu.SemaphoreType.DMA((4,)),
         ],
         compiler_params=pltpu.CompilerParams(
-            collective_id=0, has_side_effects=True, vmem_limit_bytes=60 * 2**20),
+            collective_id=0, has_side_effects=True, vmem_limit_bytes=54 * 2**20),
         cost_estimate=pl.CostEstimate(flops=7 * 10**9, bytes_accessed=2 * 10**7, transcendentals=2 * 10**6),
         name="edges",
-    )(snd, rcv, csnd, crcv, nodes, row(lists), edges, cedges, row(crcv), w1, row(b1), w2, row(b2), row(gain), row(shift))
+    )(*(pltpu.with_memory_space_constraint(v, pltpu.HBM) for v in (
+        snd, rcv, csnd, crcv, nodes, row(lists), edges, cedges, row(crcv), w1, row(b1), w2, row(b2), row(gain), row(shift))))
 
 
 def node_kernel(
     rcv,
-    rrow, edges_in, msg_in, coarse_in, inbound_in, nodes_in, w1_in, w2_in, b1, b2, gain, shift,
+    rrow, edges, msg, coarse_in, inbound_in, nodes_in, w1_in, w2_in, b1, b2, gain, shift,
     edges_out, coarse_out, nodes_out,
-    edges, msg, coarse, inbound, node_ref, w1, w2, new_nodes, fsum, wide,
-    msg_sem, edge_sem, back_sem, small_sem, node_sem,
+    coarse, inbound, node_ref, w1, w2, new_nodes, fsum, wide,
+    back_sem, small_sem, node_sem,
 ):
     steps, nsteps = msg.shape[0] // (2 * BLK), node_ref.shape[0] // BLK
     part = lambda i: pl.ds(2 * BLK * i, 2 * BLK)
-    loads = [pltpu.make_async_copy(msg_in.at[part(i)], msg.at[part(i)], msg_sem.at[i]) for i in range(steps)]
     small = [
         pltpu.make_async_copy(src, dst, small_sem.at[k]) for k, (src, dst) in enumerate((
             (nodes_in, node_ref), (w1_in, w1), (w2_in, w2), (inbound_in, inbound), (coarse_in, coarse)))
     ]
-    there = [pltpu.make_async_copy(edges_in.at[part(i)], edges.at[part(i)], edge_sem.at[i]) for i in range(steps)]
     back = [pltpu.make_async_copy(edges.at[part(i)], edges_out.at[part(i)], back_sem.at[i]) for i in range(steps)]
     back.append(pltpu.make_async_copy(coarse, coarse_out, back_sem.at[steps]))
-    for c in loads + small + there:
+    for c in small + back[:steps]:
         c.start()
     fsum[...] = jnp.zeros_like(fsum)
     for i in range(steps):
-        loads[i].wait()
         for k in (2 * i, 2 * i + 1):
             start = pl.multiple_of((rcv[k * BLK] // 8) * 8, 8)
-            ids = rrow[:, k * BLK:(k + 1) * BLK]
-            hot = (ids - start == iota((WIN, BLK), 0)).astype(F32).astype(BF)
-            fsum[pl.ds(start, WIN), :] += jnp.dot(hot, msg[k * BLK:(k + 1) * BLK, :], preferred_element_type=F32)
+            narrow = rcv[(k + 1) * BLK - 1] - start < 128
+
+            def add(rows):
+                ids = rrow[:, k * BLK:(k + 1) * BLK]
+                hot = (ids - start == iota((rows, BLK), 0)).astype(F32).astype(BF)
+                fsum[pl.ds(start, rows), :] += jnp.dot(
+                    hot, msg[k * BLK:(k + 1) * BLK, :], preferred_element_type=F32)
+
+            pl.when(narrow)(functools.partial(add, 128))
+            pl.when(jnp.logical_not(narrow))(functools.partial(add, WIN))
     for c in small:
         c.wait()
     back[steps].start()
-    for i in range(steps):
-        there[i].wait()
-        back[i].start()
-
     wide[...] = inbound[...].astype(F32)
     tags = wide[pl.ds(12, 128, stride=16), :].astype(BF)
     total = fsum[0:32, :]
@@ -400,17 +389,20 @@
     return pl.pallas_call(
         node_kernel,
         out_shape=tuple(jax.ShapeDtypeStruct(v.shape, BF) for v in (edges, coarse, nodes)),
-        in_specs=[sm, vm] + [hbm] * 7 + [vm] * 4,
+        in_specs=[sm, vm, vm, vm] + [hbm] * 5 + [vm] * 4,
         out_specs=(hbm, hbm, hbm),
-        scratch_shapes=[like(v) for v in (edges, msg, coarse, inbound, nodes, w1, w2, nodes)] + [
+        scratch_shapes=[like(v) for v in (coarse, inbound, nodes, w1, w2, nodes)] + [
             pltpu.VMEM((N + WIN, D), F32), pltpu.VMEM((2048, 128), F32),
-            pltpu.SemaphoreType.DMA((8,)), pltpu.SemaphoreType.DMA((8,)), pltpu.SemaphoreType.DMA((9,)),
+            pltpu.SemaphoreType.DMA((9,)),
             pltpu.SemaphoreType.DMA((5,)), pltpu.SemaphoreType.DMA((5,)),
         ],
-        compiler_params=pltpu.CompilerParams(vmem_limit_bytes=60 * 2**20),
+        compiler_params=pltpu.CompilerParams(vmem_limit_bytes=40 * 2**20),
         cost_estimate=pl.CostEstimate(flops=3 * 10**9, bytes_accessed=16 * 10**6, transcendentals=10**6),
         name="nodes",
-    )(rcv, row(rcv), edges, msg, coarse, inbound, nodes, w1, w2, row(b1), row(b2), row(gain), row(shift))
+    )(*(pltpu.with_memory_space_constraint(v, pltpu.HBM) for v in (rcv, row(rcv))),
+      *(pltpu.with_memory_space_constraint(v, pltpu.VMEM) for v in (edges, msg)),
+      *(pltpu.with_memory_space_constraint(v, pltpu.HBM) for v in (
+          coarse, inbound, nodes, w1, w2, row(b1), row(b2), row(gain), row(shift))))
 
 
 AXES = ("gx", "gy")

time: 58.1 us -> 56.8 us (0.978)
  Pallas kernels: 57 us -> 55.7 us
    pallas_call x1, Pallas kernels: 10.1 us -> 9.02 us  [node_call(): pl.pallas_call(node_kernel, out_shape=tuple((jax.ShapeDtypeStruct(v.shape...]
where the time goes in v6:
time: 56.8 us; the launch traced here: 56.5 us
  Pallas kernels  55.7 us (98%)
  between operations  0.8 us (1%)
    pallas_call x1, Pallas kernels, edge_call(): pl.pallas_call(edge_kernel, out_shape=(pltpu.VMEM((E, D), BF), pltpu.VMEM...  46.7 us
    pallas_call x1, Pallas kernels, node_call(): pl.pallas_call(node_kernel, out_shape=tuple((jax.ShapeDtypeStruct(v.shape...  9.02 us

profile of v6, /device:TPU:1, one launch (start us, length us, event | category | flops | bytes accessed | tf_op | source)
XLA Modules:
  0.0 56.5 jit_solution(14579666859004119348)
XLA Ops:
  0.6 46.7 %edges.1 = (bf16[4096,512]{1,0:T(8,128)(2,1)S(1)}, bf16[4096,512]{1,0:T(8,128)(2,1)S(1)}, bf16[160,512]{1,0:T(8,128)(2,1)}, bf16[128,16,128]{2,1,0:T(8,128)(2,1)}) custom-call(s32[4096]{0:T(1024)} %snd.1, s32[4096]{0:T(1024)} %rcv.3, s32[160]{0:T(256)} %csnd.1, s32[160]{0:T(256)} %crcv.1, bf16[1280,512]{1,0:T(8,128)(2,1)} %nodes_in.3, s32[1,128]{1,0:T(1,128)} %bitcast.23, ...), custom_call_target="tpu_custom_call" | custom-call | flops 7000000000 | bytes 20000000 | tf_op jit(solution)/shard_map/edges/pallas_call | solution.py:289
  47.3 9.0 %nodes.1 = (bf16[4096,512]{1,0:T(8,128)(2,1)}, bf16[160,512]{1,0:T(8,128)(2,1)}, bf16[1280,512]{1,0:T(8,128)(2,1)}) custom-call(s32[4096]{0:T(1024)} %rcv.3, s32[1,4096]{1,0:T(1,128)} %bitcast.13, bf16[4096,512]{1,0:T(8,128)(2,1)S(1)} %get-tuple-element.10.edges, bf16[4096,512]{1,0:T(8,128)(2,1)S(1)} %get-tuple-element.11.msg, ...), custom_call_target="tpu_custom_call" | custom-call | flops 3000000000 | bytes 16000000 | tf_op jit(solution)/shard_map/nodes/pallas_call | solution.py:389

commit v7 on v6

--- a/solution.py
+++ b/solution.py
@@ -14,7 +14,7 @@
 WIN = 264
 PIECES = ((0, 32), (32, 32), (64, 16))
 ORDERS = ((3, 2, 1), (2, 1, 3), (1, 3, 2))
-SEGMENTS = ((0, 1), (1, 3), (3, 4), (4, 4), (4, 5), (5, 8))
+SEGMENTS = ((0, 1), (1, 3), (3, 5), (5, 5), (5, 5), (5, 8))
 
 
 def norm_rows(x, gain, shift):

time: 56.8 us -> 56.1 us (0.988)
  Pallas kernels: 55.7 us -> 55 us
    pallas_call x1, Pallas kernels: 46.7 us -> 46 us  [edge_call(): pl.pallas_call(edge_kernel, out_shape=(pltpu.VMEM((E, D), BF), pltpu.VMEM...]
where the time goes in v7:
time: 56.1 us; the launch traced here: 55.9 us
  Pallas kernels  55 us (98%)
  between operations  0.8 us (1%)
    pallas_call x1, Pallas kernels, edge_call(): pl.pallas_call(edge_kernel, out_shape=(pltpu.VMEM((E, D), BF), pltpu.VMEM...  46 us
    pallas_call x1, Pallas kernels, node_call(): pl.pallas_call(node_kernel, out_shape=tuple((jax.ShapeDtypeStruct(v.shape...  9.03 us

profile of v7, /device:TPU:1, one launch (start us, length us, event | category | flops | bytes accessed | tf_op | source)
XLA Modules:
  0.0 55.9 jit_solution(13009429506381035720)
XLA Ops:
  0.6 46.0 %edges.1 = (bf16[4096,512]{1,0:T(8,128)(2,1)S(1)}, bf16[4096,512]{1,0:T(8,128)(2,1)S(1)}, bf16[160,512]{1,0:T(8,128)(2,1)}, bf16[128,16,128]{2,1,0:T(8,128)(2,1)}) custom-call(s32[4096]{0:T(1024)} %snd.1, s32[4096]{0:T(1024)} %rcv.3, s32[160]{0:T(256)} %csnd.1, s32[160]{0:T(256)} %crcv.1, bf16[1280,512]{1,0:T(8,128)(2,1)} %nodes_in.3, s32[1,128]{1,0:T(1,128)} %bitcast.23, ...), custom_call_target="tpu_custom_call" | custom-call | flops 7000000000 | bytes 20000000 | tf_op jit(solution)/shard_map/edges/pallas_call | solution.py:289
  46.7 9.0 %nodes.1 = (bf16[4096,512]{1,0:T(8,128)(2,1)}, bf16[160,512]{1,0:T(8,128)(2,1)}, bf16[1280,512]{1,0:T(8,128)(2,1)}) custom-call(s32[4096]{0:T(1024)} %rcv.3, s32[1,4096]{1,0:T(1,128)} %bitcast.13, bf16[4096,512]{1,0:T(8,128)(2,1)S(1)} %get-tuple-element.10.edges, bf16[4096,512]{1,0:T(8,128)(2,1)S(1)} %get-tuple-element.11.msg, ...), custom_call_target="tpu_custom_call" | custom-call | flops 3000000000 | bytes 16000000 | tf_op jit(solution)/shard_map/nodes/pallas_call | solution.py:389
